TPU v7x, 128 devices: a whole 4x4x4 slice. The times are simulated.
128 devices in a mesh: dp: 16 (over x, z), vocab: 8 (over y, core).
Axes of the slice: x: 4, y: 4, z: 4, core: 2. Of those that a mesh axis runs over, the one named last changes fastest.
Arguments:
- hidden: bfloat16 [1024, 4096], P('dp', 'vocab'), may hold values from -400 to 400
- output_head_matrix: bfloat16 [4096, 151936], P(None, ('dp', 'vocab')), may hold values from -0.09375 to 0.09375
- row_counts: int32 [16], replicated, may hold values from 1 to 64, 512 in all
- token_ids: int32 [512], P('dp'), may hold values from 0 to 151935
- segment_ids: int32 [512], P('dp'), may hold values from 0 to 31, never falling along the last dimension, each value on 1 to 64 neighbouring positions
- cotangent: float32 [512], P('dp'), may hold values from -6 to 6
Outputs:
- logprobs: float32 [512], P('dp')
- grad_hidden: bfloat16 [1024, 4096], P('dp', 'vocab')
Inputs may be any that keep to these rules, and one draw needn't show every extreme that they name: `row_counts`: live rows of each index of dp; they sum to 512, one index holds 64. `segment_ids`: never falling; each segment has 1 to 64 positions, one exactly 64.
All inputs are finite; a program needn't handle non-finite values.
Results may differ from a plain program's by a relative error of at most 0.0034.
Values may be sent and summed in bfloat16 or wider, within the bound.
No kernel may reach another device: no remote copies, remote signals or barrier semaphores. Data moves between devices by JAX's collectives and lax.ppermute only.
A program may use at most 128 MiB of HBM per device.

v0:
```python
import jax
import jax.numpy as jnp
from jax import lax
from jax.sharding import PartitionSpec as P

freq_weight = 0.4
presence_weight = 0.8


def per_device(hidden, output_head_matrix, row_counts, token_ids, segment_ids, cotangent):
    dp_count = lax.axis_size("dp")
    voc_count = lax.axis_size("vocab")
    dp_index = lax.axis_index("dp")
    slot_rows, feat_cols = hidden.shape
    per_peer = slot_rows // dp_count
    tok_rows = token_ids.shape[0]
    total_rows = tok_rows * dp_count
    voc_cols = output_head_matrix.shape[1]
    ends = jnp.cumsum(row_counts)
    starts = ends - row_counts
    my_start = starts[dp_index]
    live = jnp.arange(slot_rows, dtype=jnp.int32) < row_counts[dp_index]
    outgoing = jnp.where(live[:, None], hidden, jnp.zeros_like(hidden))
    outgoing = jnp.roll(outgoing.reshape(per_peer, dp_count, feat_cols), my_start, axis=1)
    arrived = lax.all_to_all(outgoing, "dp", split_axis=1, concat_axis=1, tiled=True)
    offsets = jnp.mod(dp_index - starts, dp_count)
    base_pos = (starts + offsets - dp_index) // dp_count
    turns = jnp.arange(per_peer, dtype=jnp.int32)[:, None]
    valid = turns * dp_count + offsets[None, :] < row_counts[None, :]
    target_position = (base_pos[None, :] + turns).reshape(-1)
    placing = (
        target_position[None, :] == jnp.arange(tok_rows, dtype=jnp.int32)[:, None]
    ) & valid.reshape(-1)[None, :]
    placing = placing.astype(jnp.bfloat16)
    packed = jnp.dot(
        placing, arrived.reshape(per_peer * dp_count, feat_cols), preferred_element_type=jnp.float32
    ).astype(jnp.bfloat16)
    gathered_token_ids, segs_all = (
        lax.all_gather(token_ids, "dp", axis=0, tiled=True),
        lax.all_gather(segment_ids, "dp", axis=0, tiled=True),
    )
    gathered_hidden_rows = lax.all_gather(packed, "dp", axis=0, tiled=True)
    logits = jnp.dot(
        lax.all_gather(gathered_hidden_rows, "vocab", axis=1, tiled=True),
        output_head_matrix,
        preferred_element_type=jnp.float32,
    )
    col_start = (dp_index * voc_count + lax.axis_index("vocab")) * voc_cols
    columns = col_start + jnp.arange(voc_cols, dtype=jnp.int32)
    hits = gathered_token_ids[:, None] == columns[None, :]
    positions = jnp.arange(total_rows, dtype=jnp.int32)
    prior_token_hits = (segs_all[:, None] == segs_all[None, :]) & (
        positions[None, :] < positions[:, None]
    )
    counts = jnp.dot(
        prior_token_hits.astype(jnp.bfloat16),
        hits.astype(jnp.bfloat16),
        preferred_element_type=jnp.float32,
    )
    scores = logits - freq_weight * counts - presence_weight * (counts > 0).astype(jnp.float32)
    picked_local = jnp.sum(jnp.where(hits, scores, jnp.zeros_like(scores)), axis=1)
    top = lax.pmax(jnp.max(scores, axis=1), ("dp", "vocab"))
    shifted = jnp.exp(scores - top[:, None])
    total, picked = lax.psum((jnp.sum(shifted, axis=1), picked_local), ("dp", "vocab"))
    all_logprobs = picked - top - jnp.log(total)
    logprobs = lax.dynamic_slice_in_dim(all_logprobs, dp_index * tok_rows, tok_rows, 0)
    residual = (hits.astype(jnp.float32) - shifted / total[:, None]).astype(jnp.bfloat16)
    head_weight_tiles = output_head_matrix.reshape(voc_count, feat_cols, voc_cols)
    blocks = tok_rows * lax.axis_size(("dp", "vocab")) // tok_rows
    span = min(dp_count, blocks // voc_count + 2)
    local_hidden_rows = residual
    local_hidden_rows = local_hidden_rows.reshape(span, tok_rows, voc_cols)
    product = jnp.einsum(
        "ubw,axw->uabx", local_hidden_rows, head_weight_tiles, preferred_element_type=jnp.float32
    )
    product = product.reshape(span * voc_count * tok_rows, feat_cols)
    summed = lax.psum_scatter(product, ("dp", "vocab"), scatter_dimension=0, tiled=True)
    scaled = (summed * cotangent[:, None]).astype(jnp.bfloat16)
    sending = jnp.dot(placing.T, scaled, preferred_element_type=jnp.float32).astype(jnp.bfloat16)
    sending = sending.reshape(per_peer, dp_count, feat_cols)
    returned = lax.all_to_all(sending, "dp", split_axis=1, concat_axis=1, tiled=True)
    grad_hidden = jnp.roll(returned, -my_start, axis=1).reshape(slot_rows, feat_cols)
    return (logprobs, grad_hidden)


def solution(mesh):
    return jax.shard_map(
        per_device,
        mesh=mesh,
        in_specs=(P("dp", "vocab"), P(None, ("dp", "vocab")), P(), P("dp"), P("dp"), P("dp")),
        out_specs=(P("dp"), P("dp", "vocab")),
        check_vma=False,
    )
```

profile of v0, /device:TPU:0, one launch (start us, length us, event | category | flops | bytes accessed | tf_op | source)
XLA Modules:
  0.0 922.9 jit_solution(9457060140498024622)
XLA Ops:
  7.2 1.2 dynamic_slice.12
  9.1 0.7 copy.18
  13.2 0.9 broadcast_select_fusion
  14.2 0.7 copy.19
  14.9 8.0 all-to-all-start
  22.9 0.7 add_compare_fusion
  23.8 6.7 all-to-all-done
  30.6 24.2 %all_gather.13 = bf16[512,512]{1,0:T(8,128)(2,1)} all-gather(bf16[32,512]{1,0:T(8,128)(2,1)S(1)} %convolution_convert_fusion.1), channel_id=1, replica_groups=mesh['dp'=16,'vocab'=8] {'dp'}, dimensions={0}, use_global_device_ids=true | all-gather | bytes 557056 | tf_op jit(solution)/shard_map/all_gather | solution.py:42
  54.9 14.1 %copy.27 = bf16[149,8,8,512]{3,2,1,0:T(8,128)(2,1)} copy(bf16[149,8,8,512]{3,1,2,0:T(8,128)(2,1)} %bitcast.30) | data formatting | bytes 19529728
  70.7 13.9 %all-reduce.2 = (s32[512]{0:T(512)S(1)}, s32[512]{0:T(512)S(1)}) all-reduce(s32[512]{0:T(512)S(1)} %dynamic-update-slice, s32[512]{0:T(512)S(1)} %dynamic-update-slice.1), channel_id=1, replica_groups=mesh['dp'=16,'vocab'=8] {'dp'}, use_global_device_ids=true, to_apply=%add | all-reduce | flops 1024 | bytes 8192
  84.7 2.4 fusion.3
  87.1 9.3 %slice_bitcast_fusion = bf16[8,512,1187]{1,0,2:T(8,128)(2,1)} fusion(bf16[1192,8,512]{2,1,0:T(8,128)(2,1)} %bitcast.29), kind=kLoop, calls=%fused_computation.3 | loop fusion | bytes 19447808 | tf_op jit(solution)/shard_map/reshape | solution.py:68
  96.4 9.7 %fusion.28 = (f32[512]{0:T(512)S(1)}, f32[512,1187]{0,1:T(8,128)S(1)}) fusion(f32[512,1187]{0,1:T(8,128)} %fusion.3, bf16[512,4096]{1,0:T(8,128)(2,1)} %all-gather.2.cloned.1.call-done, bf16[4096,1187]{0,1:T(8,128)(2,1)} %param.9), kind=kOutput, calls=%fused_computation.53 | convolution fusion | flops 4982284800 | bytes 18782208 | tf_op jit(solution)/shard_map/dot_general | solution.py:43
  106.1 63.5 %pmax.7 = f32[512]{0:T(512)S(1)} all-reduce(f32[512]{0:T(512)S(1)} %get-tuple-element.12), channel_id=1, replica_groups=mesh['dp'=16,'vocab'=8] {'dp','vocab'}, use_global_device_ids=true, to_apply=%region_4.6 | all-reduce | flops 512 | bytes 4096 | tf_op jit(solution)/shard_map/pmax | solution.py:62
  170.1 63.6 %all-reduce.3 = (f32[512]{0:T(512)S(1)}, f32[512]{0:T(512)S(1)}) all-reduce(f32[512]{0:T(512)S(1)} %get-tuple-element.4, f32[512]{0:T(512)S(1)} %get-tuple-element.3), channel_id=1, replica_groups=mesh['dp'=16,'vocab'=8] {'dp','vocab'}, use_global_device_ids=true, to_apply=%region_6.8 | all-reduce | flops 1024 | bytes 8192 | tf_op jit(solution)/shard_map/psum | solution.py:64
  233.8 1.6 fusion.8
  235.4 1.6 copy.21
  237.0 18.8 %fusion = f32[16,32,8,512]{3,1,2,0:T(8,128)} fusion(bf16[16,32,1187,1]{2,1,3,0:T(8,128)(2,1)S(1)} %bitcast.32, bf16[8,512,1187]{1,0,2:T(8,128)(2,1)} %slice_bitcast_fusion), kind=kOutput, calls=%fused_computation | convolution fusion | flops 4978638848 | bytes 19328000 | tf_op jit(solution)/shard_map/ubw,axw->uabx/dot_general | solution.py:73
  256.5 646.0 %reduce-scatter.2.cloned.1.call-done = f32[32,512]{1,0:T(8,128)} async-done(((f32[4096,512]{1,0:T(8,128)}), f32[32,512]{1,0:T(8,128)}) %reduce-scatter.2.cloned.1.call-update) | async-done | bytes 65552 | tf_op jit(solution)/shard_map/reduce_scatter | solution.py:77
  902.5 1.1 convolution_convert_fusion
  903.6 0.7 copy.23
  904.2 3.5 all-to-all-start.1
  908.4 7.0 all-to-all-done.1
  915.4 0.7 fusion.17
  (35 shorter events, 4.9 us)
Async XLA Ops:
  14.9 15.6 %all-to-all-start = ((bf16[4,16,512]{2,0,1:T(4,128)(2,1)}), bf16[4,16,512]{2,0,1:T(4,128)(2,1)S(1)}, u32[]{:S(2)}, u32[]{:S(2)}) async-start(bf16[4,16,512]{2,0,1:T(4,128)(2,1)} %copy.19), calls=%async_computation | async-start | bytes 131072 | tf_op jit(solution)/shard_map/all_to_all | solution.py:25
  22.8 73.6 %all-gather.2.cloned.1.call-start = ((), (), s32[]{:S(2)}) async-start(), calls=%async_computation.3 | async-start | bytes 4718592 | tf_op jit(solution)/shard_map/all_gather | solution.py:44
  54.8 847.6 %reduce-scatter.2.cloned.1.call-start = ((), (), s32[]{:S(2)}) async-start(), calls=%async_computation.4 | async-start | bytes 8454144 | tf_op jit(solution)/shard_map/reduce_scatter | solution.py:77
  54.9 14.1 %copy-start.3 = (u32[128]{0:T(128)S(1)}, u32[128]{0:T(128)}, u32[]{:S(2)}) copy-start(u32[128]{0:T(128)} %constant.82) | copy-start | bytes 1540
  54.9 15.3 %copy-start.1 = (s32[32]{0:T(128)S(1)}, s32[32]{0:T(128)}, u32[]{:S(2)}) copy-start(s32[32]{0:T(128)} %param.11) | copy-start | bytes 388
  54.9 15.6 %copy-start.2 = (s32[32]{0:T(128)S(1)}, s32[32]{0:T(128)}, u32[]{:S(2)}) copy-start(s32[32]{0:T(128)} %param.12) | copy-start | bytes 388
  255.9 646.6 %copy-start = (f32[32]{0:T(128)S(1)}, f32[32]{0:T(128)}, u32[]{:S(2)}) copy-start(f32[32]{0:T(128)} %param.13) | copy-start | bytes 388
  904.2 11.1 %all-to-all-start.1 = ((bf16[4,16,512]{2,0,1:T(4,128)(2,1)}), bf16[4,16,512]{2,0,1:T(4,128)(2,1)S(1)}, u32[]{:S(2)}, u32[]{:S(2)}) async-start(bf16[4,16,512]{2,0,1:T(4,128)(2,1)} %copy.23), calls=%async_computation.2 | async-start | bytes 131072 | tf_op jit(solution)/shard_map/all_to_all | solution.py:81
Sparse Core Ops, SparseCore 0:
  55.0 30.8 all-gather.1
  256.0 646.4 reduce-scatter.1
where the time goes:
time: 924 us; the launch traced here: 923 us
  waiting for transfers between devices  660 us (71%)
  blocking collectives  165 us (18%)
  matrix products  32.1 us (3%)
  local copies, waits for them, and re-layouts  30.8 us (3%)
  between operations  17.4 us (2%)
  starting transfers between devices  11.5 us (1%)
    reduce_scatter x1, waiting for transfers between devices, per_device(): lax.psum_scatter(product, ('dp', 'vocab'), scatter_dimension=0, tiled=True)  646 us
    psum x1, blocking collectives, per_device(): lax.psum((jnp.sum(shifted, axis=1), picked_local), ('dp', 'vocab'))  63.6 us
    pmax x1, blocking collectives, per_device(): top = lax.pmax(jnp.max(scores, axis=1), ('dp', 'vocab'))  63.5 us
    all_gather x1, blocking collectives, per_device(): gathered_hidden_rows = lax.all_gather(packed, 'dp', axis=0, tiled=True)  24.2 us
    dot_general x1, matrix products, per_device(): jnp.einsum('ubw,axw->uabx', local_hidden_rows, head_weight_tiles, preferr...  18.8 us
  transfers between devices with their start and end apart: 4, of which 3 were waited for; matrix products, arithmetic and copies ran while one was open for 3% of the time, Pallas kernels for 0%

commit v1 on v0

v1 whole, which is shorter than its diff:
```python
import functools

import jax
import jax.numpy as jnp
from jax import lax
from jax.experimental import pallas as pl
from jax.experimental.pallas import tpu as pltpu
from jax.sharding import PartitionSpec as P

freq_weight = 0.4
presence_weight = 0.8

N_DP, N_VOC = 16, 8
FEAT = 512
BF, F32, I32 = jnp.bfloat16, jnp.float32, jnp.int32
MIB = 1 << 20


def params(limit=32):
    return pltpu.CompilerParams(vmem_limit_bytes=limit * MIB)


def coords():
    dp, voc = lax.axis_index("dp"), lax.axis_index("vocab")
    return dp // 4, lax.rem(dp, 4), voc // 2, lax.rem(voc, 2)


def flat(x, z, y, c):
    return x * 32 + z * 8 + y * 2 + c


def shift_perm(axes, k):
    pairs = []
    for x in range(4):
        for z in range(4):
            for y in range(4):
                for c in range(2):
                    to = dict(x=x, z=z, y=y, c=c)
                    to[axes[c]] = (to[axes[c]] + k) % 4
                    pairs.append((flat(x, z, y, c), flat(**to)))
    return pairs


CORE_PERM = [(i, i ^ 1) for i in range(N_DP * N_VOC)]


def permute(v, pairs):
    return lax.ppermute(v, ("dp", "vocab"), pairs)


def iota(shape, dim):
    return lax.broadcasted_iota(I32, shape, dim)


VM = pl.BlockSpec(memory_space=pltpu.VMEM)
SM = pl.BlockSpec(memory_space=pltpu.SMEM)
ANY = pl.BlockSpec(memory_space=pl.ANY)


def my_start(rc_ref, dp):
    start = jnp.int32(0)
    for s in range(N_DP):
        start = start + jnp.where(s < dp, rc_ref[s], 0)
    return start


def pack_kernel(rc_ref, hid_ref, tok_ref, seg_ref, out_ref):
    dp = lax.axis_index("dp")
    start, count = my_start(rc_ref, dp), rc_ref[dp]
    row, col = iota((128, 64), 0), iota((128, 64), 1)
    t = row & 7
    src = t * N_DP + (((row >> 3) - start) & 15)
    sel = (t < 4) & (col == src) & (col < count)
    out_ref[...] = jnp.dot(sel.astype(F32).astype(BF), hid_ref[...], preferred_element_type=F32).astype(BF)
    t32 = iota((128, 32), 0) & 7
    tok, seg = tok_ref[...], seg_ref[...]
    digit = jnp.where(t32 == 4, tok & 255, jnp.where(t32 == 5, (tok >> 8) & 255, jnp.where(t32 == 6, tok >> 16, seg)))
    old = out_ref[:, 0:32].astype(F32)
    out_ref[:, 0:32] = jnp.where(t32 >= 4, digit.astype(F32), old).astype(BF)


def placing(rc_ref, shape, slot_dim):
    dp = lax.axis_index("dp")
    k, pos = iota(shape, slot_dim), iota(shape, 1 - slot_dim)
    s, t = k >> 3, k & 7
    start = jnp.zeros(shape, I32)
    count = jnp.zeros(shape, I32)
    run = jnp.int32(0)
    for i in range(N_DP):
        start = jnp.where(s == i, run, start)
        count = jnp.where(s == i, rc_ref[i], count)
        run = run + rc_ref[i]
    offset = (dp - start) & 15
    base = (start + offset - dp) >> 4
    sel = (t < 4) & (t * N_DP + offset < count) & (base + t == pos)
    return sel.astype(F32).astype(BF)


def unpack_kernel(rc_ref, arr_ref, out_ref):
    sel = placing(rc_ref, (32, 128), 1)
    out_ref[...] = jnp.dot(sel, arr_ref[...], preferred_element_type=F32).astype(BF)


def place_kernel(mode, a0, a1, a2, a3, out_ref):
    x, z, y, c = coords()
    own = z if mode == "z" else jnp.where(c == 0, x, y)
    for d, a in enumerate((a0, a1, a2, a3)):
        out_ref[pl.ds((own + d) & 3, 1)] = a[...][None]


def column(row):
    wide = jnp.broadcast_to(row, (128, row.shape[1]))
    return jnp.transpose(wide)[:, 0:1]


def code_kernel(cols, tok_ref, seg_ref, out_ref):
    dp, voc = lax.axis_index("dp"), lax.axis_index("vocab")
    tok, seg = tok_ref[...], seg_ref[...]
    tok_col = column(tok.astype(F32)).astype(I32)
    seg_col = column(seg.astype(F32)).astype(I32)
    prior = (seg_col == seg) & (iota((512, 512), 1) < iota((512, 512), 0))
    prior = prior.astype(F32).astype(BF)
    first = (dp * N_VOC + voc) * cols
    hits = (tok_col == first + iota((512, cols), 1)).astype(F32)
    counts = jnp.dot(prior, hits.astype(BF), preferred_element_type=F32)
    out_ref[...] = (counts + 128.0 * hits).astype(BF)


def scores_kernel(cols, *refs):
    blocks, (w_ref, code_ref, s_ref, stat_ref, xs, ws, ss, xsem, wsem) = refs[:8], refs[8:]
    x, z, y, c = coords()
    for k in range(4):
        pltpu.make_async_copy(w_ref.at[pl.ds(k * 1024, 1024)], ws.at[k], wsem.at[k]).start()
    copies = []
    for n in range(8):
        core = c if n < 4 else 1 - c
        own = jnp.where(core == 0, y, x)
        p = (own + n % 4) & 3
        for q in range(4):
            xx = jnp.where(core == 0, q, p)
            yy = jnp.where(core == 0, p, q)
            dst = xs.at[pl.ds(pl.multiple_of(xx * 128, 128), 128), pl.ds(pl.multiple_of((yy * 2 + core) * FEAT, FEAT), FEAT)]
            copies.append(pltpu.make_async_copy(blocks[n].at[q], dst, xsem.at[n * 4 + q]))
    for cp in copies:
        cp.start()
    for cp in copies:
        cp.wait()
    for k in range(4):
        pltpu.make_async_copy(w_ref.at[pl.ds(k * 1024, 1024)], ws.at[k], wsem.at[k]).wait()
        part = jnp.dot(xs[:, k * 1024:(k + 1) * 1024], ws[k], preferred_element_type=F32)
        if k == 0:
            s_ref[...] = part
        else:
            s_ref[...] += part

    def rows(i, _):
        at = pl.ds(pl.multiple_of(i * 32, 32), 32)
        code = code_ref[at, :].astype(F32)
        hit = code > 127.5
        counts = jnp.where(hit, code - 128.0, code)
        s = s_ref[at, :] - freq_weight * counts - presence_weight * (counts > 0).astype(F32)
        s_ref[at, :] = s
        m = jnp.max(s, axis=1, keepdims=True)
        ss[at, 0:1] = m
        ss[at, 1:2] = jnp.sum(jnp.exp(s - m), axis=1, keepdims=True)
        ss[at, 2:3] = jnp.sum(jnp.where(hit, s, 0.0), axis=1, keepdims=True)
        return _

    lax.fori_loop(0, 16, rows, 0)
    flat_stats = jnp.transpose(ss[...])
    for j in range(3):
        for k in range(4):
            piece = flat_stats[j:j + 1, k * 128:(k + 1) * 128]
            for n in range(N_VOC):
                stat_ref[n, j * 4 + k:j * 4 + k + 1, :] = piece
    for n in range(N_VOC):
        stat_ref[n, 12:16, :] = jnp.zeros((4, 128), F32)


def merge(st_ref, n):
    m = st_ref[0, 0:4, :]
    for i in range(1, n):
        m = jnp.maximum(m, st_ref[i, 0:4, :])
    total = jnp.zeros_like(m)
    picked = jnp.zeros_like(m)
    for i in range(n):
        total = total + st_ref[i, 4:8, :] * jnp.exp(st_ref[i, 0:4, :] - m)
        picked = picked + st_ref[i, 8:12, :]
    return m, total, picked


def merge_kernel(st_ref, out_ref):
    m, total, picked = merge(st_ref, N_VOC)
    for n in range(N_DP):
        out_ref[n, 0:4, :] = m
        out_ref[n, 4:8, :] = total
        out_ref[n, 8:12, :] = picked
        out_ref[n, 12:16, :] = jnp.zeros((4, 128), F32)


def grad_kernel(cols, w_ref, s_ref, code_ref, st_ref, keep_ref, send_ref, lp_ref, ws, rs, cs, lps, wsem):
    x, z, y, c = coords()

    def head(i):
        block = (i & 3) * 2 + jnp.where(i < 4, 1 - c, c)
        return pltpu.make_async_copy(w_ref.at[pl.ds(pl.multiple_of(block * FEAT, FEAT), FEAT)], ws.at[i], wsem.at[i])

    for i in range(8):
        head(i).start()
    m, total, picked = merge(st_ref, N_DP)
    lps[0:4, :] = picked - m - jnp.log(total)
    mine = lps[pl.ds(x, 1), :]
    mine = pltpu.roll(mine, (128 - 32 * z) & 127, 1)
    lp_ref[...] = mine[:, 0:32]
    for k in range(4):
        cs[k * 128:(k + 1) * 128, 0:128] = jnp.transpose(jnp.broadcast_to(m[k:k + 1, :], (128, 128)))
        cs[k * 128:(k + 1) * 128, 128:256] = jnp.transpose(jnp.broadcast_to(total[k:k + 1, :], (128, 128)))

    def rows(i, _):
        at = pl.ds(pl.multiple_of(i * 32, 32), 32)
        hit = (code_ref[at, :].astype(F32) > 127.5).astype(F32)
        p = jnp.exp(s_ref[at, :] - cs[at, 0:1]) / cs[at, 128:129]
        rs[at, :] = (hit - p).astype(BF)
        return _

    lax.fori_loop(0, 16, rows, 0)

    def product(i):
        return lax.dot_general(rs[...], ws[i], (((1,), (1,)), ((), ())), preferred_element_type=F32)

    for half, core, out_ref in ((0, 1 - c, send_ref), (4, c, keep_ref)):
        for yy in range(4):
            head(half + yy).wait()
            v = product(half + yy)
            for xx in range(4):
                p = jnp.where(core == 0, yy, xx)
                q = jnp.where(core == 0, xx, yy)
                out_ref[p, q] = v[xx * 128:(xx + 1) * 128].astype(out_ref.dtype)


def core_sum_kernel(keep_ref, got_ref, own_ref, b1, b2, b3):
    x, z, y, c = coords()
    own = jnp.where(c == 0, y, x)
    for d, out in enumerate((own_ref, b1, b2, b3)):
        p = (own + d) & 3
        for q in range(4):
            out[q] = (keep_ref[p, q] + got_ref[p, q].astype(F32)).astype(out.dtype)


def ring_sum_kernel(mode, own_in, r1, r2, r3, own_ref, b1, b2, b3):
    x, z, y, c = coords()
    own = z if mode == "z" else jnp.where(c == 0, x, y)
    for d, out in enumerate((own_ref, b1, b2, b3)):
        q = (own + d) & 3
        v = own_in[q].astype(F32) + r1[q].astype(F32) + r2[q].astype(F32) + r3[q].astype(F32)
        out[...] = v.astype(out.dtype)


def return_kernel(rc_ref, cot_ref, own_in, r1, r2, r3, out_ref):
    v = own_in[...] + r1[...] + r2[...] + r3[...]
    scaled = (v * cot_ref[...]).astype(BF)
    sel = placing(rc_ref, (128, 32), 0)
    out_ref[...] = jnp.dot(sel, scaled, preferred_element_type=F32).astype(BF)


def slots_kernel(rc_ref, arr_ref, out_ref):
    dp = lax.axis_index("dp")
    start, count = my_start(rc_ref, dp), rc_ref[dp]
    j, k = iota((64, 128), 0), iota((64, 128), 1)
    at = ((start + j) & 15) * 8 + (j >> 4)
    sel = ((k == at) & (j < count)).astype(F32).astype(BF)
    out_ref[...] = jnp.dot(sel, arr_ref[...], preferred_element_type=F32).astype(BF)


def sds(shape, dtype):
    return jax.ShapeDtypeStruct(shape, dtype)


def call(kernel, ins, outs, in_specs=None, scratch=(), limit=32, cost=None):
    multi = isinstance(outs, (list, tuple))
    return pl.pallas_call(
        kernel,
        out_shape=outs,
        in_specs=in_specs or [VM] * len(ins),
        out_specs=[VM] * len(outs) if multi else VM,
        scratch_shapes=list(scratch),
        compiler_params=params(limit),
        cost_estimate=cost,
    )(*ins)


def cost(flops, nbytes):
    return pl.CostEstimate(flops=flops, bytes_accessed=nbytes, transcendentals=0)


def per_device(hidden, head, row_counts, token_ids, segment_ids, cotangent):
    cols = head.shape[1]
    outgoing = call(
        pack_kernel,
        (row_counts, hidden, token_ids.reshape(1, 32), segment_ids.reshape(1, 32)),
        sds((128, FEAT), BF),
        in_specs=[SM, VM, VM, VM],
    )
    arrived = lax.all_to_all(outgoing.reshape(N_DP, 8, FEAT), "dp", 0, 0, tiled=True)
    flat_arrived = arrived.reshape(128, FEAT)
    packed = call(unpack_kernel, (row_counts, flat_arrived), sds((32, FEAT), BF), in_specs=[SM, VM])
    digits = arrived[:, 4:8, 0:32].astype(F32)
    tokens = (digits[:, 0] + 256.0 * digits[:, 1] + 65536.0 * digits[:, 2]).astype(I32).reshape(1, 512)
    segments = digits[:, 3].astype(I32).reshape(1, 512)

    first = [packed] + [permute(packed, shift_perm("zz", 4 - d)) for d in (1, 2, 3)]
    g1 = call(functools.partial(place_kernel, "z"), first, sds((4, 32, FEAT), BF)).reshape(128, FEAT)
    second = [g1] + [permute(g1, shift_perm("xy", 4 - d)) for d in (1, 2, 3)]
    g2 = call(functools.partial(place_kernel, "xy"), second, sds((4, 128, FEAT), BF))
    third = [g2] + [permute(g2, shift_perm("yx", 4 - d)) for d in (1, 2, 3)]
    other = [permute(v, CORE_PERM) for v in third]
    code = call(
        functools.partial(code_kernel, cols), (tokens, segments), sds((512, cols), BF), cost=cost(2 * 512 * 512 * 1280, 3 * MIB)
    )

    s, stats = call(
        functools.partial(scores_kernel, cols),
        (*third, *other, head, code),
        [sds((512, cols), F32), sds((N_VOC, 16, 128), F32)],
        in_specs=[ANY] * 9 + [VM],
        scratch=[
            pltpu.VMEM((512, 4096), BF),
            pltpu.VMEM((4, 1024, cols), BF),
            pltpu.VMEM((512, 128), F32),
            pltpu.SemaphoreType.DMA((32,)),
            pltpu.SemaphoreType.DMA((4,)),
        ],
        limit=40,
        cost=cost(2 * 512 * 4096 * 1280, 16 * MIB),
    )
    stats = lax.all_to_all(stats, "vocab", 0, 0, tiled=True)
    stats = call(merge_kernel, (stats,), sds((N_DP, 16, 128), F32))
    stats = lax.all_to_all(stats, "dp", 0, 0, tiled=True)

    keep, send, logprobs = call(
        functools.partial(grad_kernel, cols),
        (head, s, code, stats),
        [sds((4, 4, 128, FEAT), F32), sds((4, 4, 128, FEAT), BF), sds((1, 32), F32)],
        in_specs=[ANY, VM, VM, VM],
        scratch=[
            pltpu.VMEM((8, FEAT, cols), BF),
            pltpu.VMEM((512, cols), BF),
            pltpu.VMEM((512, 256), F32),
            pltpu.VMEM((8, 128), F32),
            pltpu.SemaphoreType.DMA((8,)),
        ],
        limit=48,
        cost=cost(2 * 512 * 4096 * 1280, 16 * MIB),
    )
    got = permute(send, CORE_PERM)
    own, *out = call(
        core_sum_kernel, (keep, got), [sds((4, 128, FEAT), F32)] + [sds((4, 128, FEAT), BF)] * 3
    )
    got = [permute(v, shift_perm("yx", d + 1)) for d, v in enumerate(out)]
    own, *out = call(
        functools.partial(ring_sum_kernel, "xy"), (own, *got), [sds((128, FEAT), F32)] + [sds((128, FEAT), F32)] * 3
    )
    got = [permute(v, shift_perm("xy", d + 1)) for d, v in enumerate(out)]
    own, *out = call(
        functools.partial(ring_sum_kernel, "z"),
        [v.reshape(4, 32, FEAT) for v in (own, *got)],
        [sds((32, FEAT), F32)] * 4,
    )
    got = [permute(v, shift_perm("zz", d + 1)) for d, v in enumerate(out)]
    returning = call(
        return_kernel,
        (row_counts, cotangent.reshape(32, 1), own, *got),
        sds((128, FEAT), BF),
        in_specs=[SM] + [VM] * 5,
    )
    returned = lax.all_to_all(returning.reshape(N_DP, 8, FEAT), "dp", 0, 0, tiled=True)
    grad_hidden = call(
        slots_kernel, (row_counts, returned.reshape(128, FEAT)), sds((64, FEAT), BF), in_specs=[SM, VM]
    )
    return logprobs.reshape(32), grad_hidden


def solution(mesh):
    return jax.shard_map(
        per_device,
        mesh=mesh,
        in_specs=(P("dp", "vocab"), P(None, ("dp", "vocab")), P(), P("dp"), P("dp"), P("dp")),
        out_specs=(P("dp"), P("dp", "vocab")),
        check_vma=False,
    )
```

time: 924 us -> 176 us (0.19)
  waiting for transfers between devices: 660 us -> 53.8 us
  blocking collectives: 165 us -> 46.7 us
  Pallas kernels: 0 us -> 32.5 us
  matrix products: 32.1 us -> 0 us
  between operations: 17.4 us -> 0.79 us
  local copies, waits for them, and re-layouts: 30.8 us -> 19.4 us
  starting transfers between devices: 11.5 us -> 22.3 us
    reduce_scatter x1 -> x0, waiting for transfers between devices: 646 us -> none  [per_device(): lax.psum_scatter(product, ('dp', 'vocab'), scatter_dimension=0, tiled=True)]
    psum x1 -> x0, blocking collectives: 63.6 us -> none  [per_device(): lax.psum((jnp.sum(shifted, axis=1), picked_local), ('dp', 'vocab'))]
    pmax x1 -> x0, blocking collectives: 63.5 us -> none  [per_device(): top = lax.pmax(jnp.max(scores, axis=1), ('dp', 'vocab'))]
    ppermute x0 -> x23, waiting for transfers between devices: none -> 53.8 us  [permute(): return lax.ppermute(v, ('dp', 'vocab'), pairs)]
    all_to_all x0 -> x4, blocking collectives: none -> 46.7 us  [the longest x1 15.6 us: per_device(): lax.all_to_all(outgoing.reshape(N_DP, 8, FEAT), 'dp', 0, 0, tiled=True)]
    pallas_call x0 -> x13, Pallas kernels: none -> 32.5 us  [call(): pl.pallas_call(kernel, out_shape=outs, in_specs=in_specs or [VM] * len(in...]
    dot_general x5 -> x0, matrix products: 32.1 us -> none  [the longest x1 18.8 us: per_device(): jnp.einsum('ubw,axw->uabx', local_hidden_rows, head_weight_tiles, preferr...]
    all_gather x1 -> x0, blocking collectives: 24.2 us -> none  [per_device(): gathered_hidden_rows = lax.all_gather(packed, 'dp', axis=0, tiled=True)]
  transfers between devices with their start and end apart: 4 -> 23, of which waited for: 3 -> 16; matrix products, arithmetic and copies ran while one was open for 3% -> 8% of each run, Pallas kernels for 0% -> 1%
where the time goes in v1:
time: 176 us
  waiting for transfers between devices  53.8 us (31%)
  blocking collectives  46.7 us (27%)
  Pallas kernels  32.5 us (18%)
  starting transfers between devices  22.3 us (13%)
  local copies, waits for them, and re-layouts  19.4 us (11%)
    ppermute x23, waiting for transfers between devices, permute(): return lax.ppermute(v, ('dp', 'vocab'), pairs)  53.8 us
    pallas_call x13, Pallas kernels, call(): pl.pallas_call(kernel, out_shape=outs, in_specs=in_specs or [VM] * len(in...  32.5 us
    ppermute x23, starting transfers between devices, permute(): return lax.ppermute(v, ('dp', 'vocab'), pairs)  22.3 us
    unnamed x15, local copies, waits for them, and re-layouts  19.2 us
    all_to_all x1, blocking collectives, per_device(): lax.all_to_all(outgoing.reshape(N_DP, 8, FEAT), 'dp', 0, 0, tiled=True)  15.6 us
    all_to_all x1, blocking collectives, per_device(): lax.all_to_all(returning.reshape(N_DP, 8, FEAT), 'dp', 0, 0, tiled=True)  12.3 us
    all_to_all x1, blocking collectives, per_device(): stats = lax.all_to_all(stats, 'dp', 0, 0, tiled=True)  10.8 us
    all_to_all x1, blocking collectives, per_device(): stats = lax.all_to_all(stats, 'vocab', 0, 0, tiled=True)  8 us
  transfers between devices with their start and end apart: 23, of which 16 were waited for; matrix products, arithmetic and copies ran while one was open for 8% of the time, Pallas kernels for 1%

profile of v1, /device:TPU:0, one launch (start us, length us, event | category | flops | bytes accessed | tf_op | source)
XLA Modules:
  0.0 175.5 jit_solution(5732906645045348597)
XLA Ops:
  4.2 15.6 %all_to_all.20 = bf16[16,8,512]{2,1,0:T(8,128)(2,1)S(1)} all-to-all(bf16[16,8,512]{2,1,0:T(8,128)(2,1)S(1)} %bitcast.16), channel_id=1, replica_groups=mesh['dp'=16,'vocab'=8] {'dp'}, dimensions={0} | all-to-all | bytes 262144 | tf_op jit(solution)/shard_map/all_to_all | solution.py:304
  24.4 2.8 %collective-permute-done.1.a2 = bf16[32,512]{1,0:T(8,128)(2,1)S(1)} collective-permute-done((bf16[32,512]{1,0:T(8,128)(2,1)S(1)}, bf16[32,512]{1,0:T(8,128)(2,1)S(1)}, u32[]{:S(2)}, u32[]{:S(2)}) %collective-permute-start.1) | collective-permute-done | bytes 32800 | tf_op jit(solution)/shard_map/ppermute | solution.py:48
  29.4 1.4 collective-permute-start.4
  30.9 2.3 %collective-permute-done.3.a1 = bf16[128,512]{1,0:T(8,128)(2,1)S(1)} collective-permute-done((bf16[128,512]{1,0:T(8,128)(2,1)S(1)}, bf16[128,512]{1,0:T(8,128)(2,1)S(1)}, u32[]{:S(2)}, u32[]{:S(2)}) %collective-permute-start.3) | collective-permute-done | bytes 131104 | tf_op jit(solution)/shard_map/ppermute | solution.py:48
  33.2 2.7 %collective-permute-done.4.a2 = bf16[128,512]{1,0:T(8,128)(2,1)S(1)} collective-permute-done((bf16[128,512]{1,0:T(8,128)(2,1)S(1)}, bf16[128,512]{1,0:T(8,128)(2,1)S(1)}, u32[]{:S(2)}, u32[]{:S(2)}) %collective-permute-start.4) | collective-permute-done | bytes 131104 | tf_op jit(solution)/shard_map/ppermute | solution.py:48
  35.9 1.4 collective-permute-done.5.a3
  37.3 3.1 %collective-permute-start.6 = (bf16[4,128,512]{2,1,0:T(8,128)(2,1)S(1)}, bf16[4,128,512]{2,1,0:T(8,128)(2,1)S(1)}, u32[]{:S(2)}, u32[]{:S(2)}) collective-permute-start(bf16[4,128,512]{2,1,0:T(8,128)(2,1)S(1)} %shard_map.80.refs_0_), channel_id=1, source_target_pairs={{0,6},{1,97},{2,0},{3,99},{4,2},{5,101},{6,4},{7,103},{8,14},{9,10... | collective-permute-start | bytes 1572872 | tf_op jit(solution)/shard_map/ppermute | solution.py:48
  42.1 10.6 %collective-permute-done.6.refs_1_ = bf16[4,128,512]{2,1,0:T(8,128)(2,1)S(1)} collective-permute-done((bf16[4,128,512]{2,1,0:T(8,128)(2,1)S(1)}, bf16[4,128,512]{2,1,0:T(8,128)(2,1)S(1)}, u32[]{:S(2)}, u32[]{:S(2)}) %collective-permute-start.6) | collective-permute-done | bytes 524320 | tf_op jit(solution)/shard_map/ppermute | solution.py:48
  53.2 3.5 %collective-permute-done.8.refs_3_ = bf16[4,128,512]{2,1,0:T(8,128)(2,1)S(1)} collective-permute-done((bf16[4,128,512]{2,1,0:T(8,128)(2,1)S(1)}, bf16[4,128,512]{2,1,0:T(8,128)(2,1)S(1)}, u32[]{:S(2)}, u32[]{:S(2)}) %collective-permute-start.8) | collective-permute-done | bytes 524320 | tf_op jit(solution)/shard_map/ppermute | solution.py:48
  56.7 14.2 %copy.14.refs_8_.w_ref = bf16[4096,1187]{1,0:T(8,128)(2,1)} copy(bf16[4096,1187]{0,1:T(8,128)(2,1)} %param.7) | data formatting | bytes 19447808 | tf_op args[1]
  71.2 1.4 shard_map.81.refs_9_.code_ref
  72.6 15.7 %shard_map.82 = (f32[512,1187]{1,0:T(8,128)S(1)}, f32[8,16,128]{2,1,0:T(8,128)S(1)}) custom-call(bf16[4,128,512]{2,1,0:T(8,128)(2,1)S(1)} %shard_map.80.refs_0_, bf16[4,128,512]{2,1,0:T(8,128)(2,1)S(1)} %collective-permute-done.6.refs_1_, bf16[4,128,512]{2,1,0:T(8,128)(2,1)S(1)} %collective-permute-done.7.refs_2_, ...), custom_call_target="tpu_custom_call" | custom-call | flops 5368709120 | bytes 16777216 | tf_op jit(solution)/shard_map/pallas_call | solution.py:281
  88.3 8.0 %all_to_all.21.st_ref = f32[8,16,128]{2,1,0:T(8,128)S(1)} all-to-all(f32[8,16,128]{2,1,0:T(8,128)S(1)} %get-tuple-element.20), channel_id=1, replica_groups=mesh['dp'=16,'vocab'=8] {'vocab'}, dimensions={0} | all-to-all | bytes 131072 | tf_op jit(solution)/shard_map/all_to_all | solution.py:336
  96.3 10.8 %all_to_all.22.st_ref = f32[16,16,128]{2,1,0:T(8,128)S(1)} all-to-all(f32[16,16,128]{2,1,0:T(8,128)S(1)} %shard_map.83), channel_id=1, replica_groups=mesh['dp'=16,'vocab'=8] {'dp'}, dimensions={0} | all-to-all | bytes 262144 | tf_op jit(solution)/shard_map/all_to_all | solution.py:338
  107.1 11.2 %shard_map.84 = (f32[4,4,128,512]{3,2,1,0:T(8,128)}, bf16[4,4,128,512]{3,2,1,0:T(8,128)(2,1)S(1)}, f32[1,32]{1,0:T(1,128)}) custom-call(bf16[4096,1187]{1,0:T(8,128)(2,1)} %copy.14.refs_8_.w_ref, f32[512,1187]{1,0:T(8,128)S(1)} %get-tuple-element.19.s_ref, bf16[512,1187]{1,0:T(8,128)(2,1)S(1)} %shard_map.81.refs_9_.code_ref, ...), custom_call_target="tpu_custom_call" | custom-call | flops 5368709120 | bytes 16777216 | tf_op jit(solution)/shard_map/pallas_call | solution.py:281
  118.4 4.1 %collective-permute-done.13.got_ref = bf16[4,4,128,512]{3,2,1,0:T(8,128)(2,1)S(1)} collective-permute-done((bf16[4,4,128,512]{3,2,1,0:T(8,128)(2,1)S(1)}, bf16[4,4,128,512]{3,2,1,0:T(8,128)(2,1)S(1)}, u32[]{:S(2)}, u32[]{:S(2)}) %collective-permute-start.13) | collective-permute-done | bytes 2097184 | tf_op jit(solution)/shard_map/ppermute | solution.py:48
  122.6 2.2 %copy-done = f32[4,4,128,512]{3,2,1,0:T(8,128)S(1)} copy-done((f32[4,4,128,512]{3,2,1,0:T(8,128)S(1)}, f32[4,4,128,512]{3,2,1,0:T(8,128)}, u32[]{:S(2)}) %copy-start) | copy-done | bytes 4194328
  125.8 2.1 %collective-permute-start.15 = (bf16[4,128,512]{2,1,0:T(8,128)(2,1)S(1)}, bf16[4,128,512]{2,1,0:T(8,128)(2,1)S(1)}, u32[]{:S(2)}, u32[]{:S(2)}) collective-permute-start(bf16[4,128,512]{2,1,0:T(8,128)(2,1)S(1)} %get-tuple-element.26), channel_id=1, source_target_pairs={{0,4},{1,65},{2,6},{3,67},{4,0},{5,69},{6,2},{7,71},{8,12},{9,73},... | collective-permute-start | bytes 1572872 | tf_op jit(solution)/shard_map/ppermute | solution.py:48
  128.8 12.4 %collective-permute-done.14.r1 = bf16[4,128,512]{2,1,0:T(8,128)(2,1)S(1)} collective-permute-done((bf16[4,128,512]{2,1,0:T(8,128)(2,1)S(1)}, bf16[4,128,512]{2,1,0:T(8,128)(2,1)S(1)}, u32[]{:S(2)}, u32[]{:S(2)}) %collective-permute-start.14) | collective-permute-done | bytes 524320 | tf_op jit(solution)/shard_map/ppermute | solution.py:48
  145.7 3.1 %collective-permute-done.19 = f32[128,512]{1,0:T(8,128)S(1)} collective-permute-done((f32[128,512]{1,0:T(8,128)S(1)}, f32[128,512]{1,0:T(8,128)S(1)}, u32[]{:S(2)}, u32[]{:S(2)}) %collective-permute-start.19) | collective-permute-done | bytes 262176 | tf_op jit(solution)/shard_map/ppermute | solution.py:48
  148.7 5.2 %collective-permute-done.17 = f32[128,512]{1,0:T(8,128)S(1)} collective-permute-done((f32[128,512]{1,0:T(8,128)S(1)}, f32[128,512]{1,0:T(8,128)S(1)}, u32[]{:S(2)}, u32[]{:S(2)}) %collective-permute-start.17) | collective-permute-done | bytes 262176 | tf_op jit(solution)/shard_map/ppermute | solution.py:48
  154.5 2.1 %collective-permute-start.21 = (f32[32,512]{1,0:T(8,128)S(1)}, f32[32,512]{1,0:T(8,128)S(1)}, u32[]{:S(2)}, u32[]{:S(2)}) collective-permute-start(f32[32,512]{1,0:T(8,128)S(1)} %get-tuple-element.34), channel_id=1, source_target_pairs={{0,16},{1,17},{2,18},{3,19},{4,20},{5,21},{6,22},{7,23},{8,24},{9,... | collective-permute-start | bytes 196616 | tf_op jit(solution)/shard_map/ppermute | solution.py:48
  156.6 1.5 collective-permute-start.22
  161.9 12.3 %all_to_all.23 = bf16[16,8,512]{2,1,0:T(8,128)(2,1)S(1)} all-to-all(bf16[16,8,512]{2,1,0:T(8,128)(2,1)S(1)} %bitcast.14), channel_id=1, replica_groups=mesh['dp'=16,'vocab'=8] {'dp'}, dimensions={0} | all-to-all | bytes 262144 | tf_op jit(solution)/shard_map/all_to_all | solution.py:376
  (59 shorter events, 25.3 us)
Async XLA Ops:
  20.5 3.9 %collective-permute-start = (bf16[32,512]{1,0:T(8,128)(2,1)S(1)}, bf16[32,512]{1,0:T(8,128)(2,1)S(1)}, u32[]{:S(2)}, u32[]{:S(2)}) collective-permute-start(bf16[32,512]{1,0:T(8,128)(2,1)S(1)} %shard_map.78.a0), channel_id=1, source_target_pairs={{0,24},{1,25},{2,26},{3,27},{4,28},{5,29},{6,30},{7,31},{8,0},{9,1... | collective-permute-start | bytes 98312 | tf_op jit(solution)/shard_map/ppermute | solution.py:48
  21.7 5.4 %collective-permute-start.1 = (bf16[32,512]{1,0:T(8,128)(2,1)S(1)}, bf16[32,512]{1,0:T(8,128)(2,1)S(1)}, u32[]{:S(2)}, u32[]{:S(2)}) collective-permute-start(bf16[32,512]{1,0:T(8,128)(2,1)S(1)} %shard_map.78.a0), channel_id=1, source_target_pairs={{0,16},{1,17},{2,18},{3,19},{4,20},{5,21},{6,22},{7,23},{8,24},{9,... | collective-permute-start | bytes 98312 | tf_op jit(solution)/shard_map/ppermute | solution.py:48
  23.0 5.1 %collective-permute-start.2 = (bf16[32,512]{1,0:T(8,128)(2,1)S(1)}, bf16[32,512]{1,0:T(8,128)(2,1)S(1)}, u32[]{:S(2)}, u32[]{:S(2)}) collective-permute-start(bf16[32,512]{1,0:T(8,128)(2,1)S(1)} %shard_map.78.a0), channel_id=1, source_target_pairs={{0,8},{1,9},{2,10},{3,11},{4,12},{5,13},{6,14},{7,15},{8,16},{9,17... | collective-permute-start | bytes 98312 | tf_op jit(solution)/shard_map/ppermute | solution.py:48
  28.2 5.0 %collective-permute-start.3 = (bf16[128,512]{1,0:T(8,128)(2,1)S(1)}, bf16[128,512]{1,0:T(8,128)(2,1)S(1)}, u32[]{:S(2)}, u32[]{:S(2)}) collective-permute-start(bf16[128,512]{1,0:T(8,128)(2,1)S(1)} %bitcast.17), channel_id=1, source_target_pairs={{0,96},{1,7},{2,98},{3,1},{4,100},{5,3},{6,102},{7,5},{8,104},{9,1... | collective-permute-start | bytes 393224 | tf_op jit(solution)/shard_map/ppermute | solution.py:48
  29.4 6.5 %collective-permute-start.4 = (bf16[128,512]{1,0:T(8,128)(2,1)S(1)}, bf16[128,512]{1,0:T(8,128)(2,1)S(1)}, u32[]{:S(2)}, u32[]{:S(2)}) collective-permute-start(bf16[128,512]{1,0:T(8,128)(2,1)S(1)} %bitcast.18), channel_id=1, source_target_pairs={{0,64},{1,5},{2,66},{3,7},{4,68},{5,1},{6,70},{7,3},{8,72},{9,13},... | collective-permute-start | bytes 393224 | tf_op jit(solution)/shard_map/ppermute | solution.py:48
  30.8 6.5 %collective-permute-start.5 = (bf16[128,512]{1,0:T(8,128)(2,1)S(1)}, bf16[128,512]{1,0:T(8,128)(2,1)S(1)}, u32[]{:S(2)}, u32[]{:S(2)}) collective-permute-start(bf16[128,512]{1,0:T(8,128)(2,1)S(1)} %bitcast.19), channel_id=1, source_target_pairs={{0,32},{1,3},{2,34},{3,5},{4,36},{5,7},{6,38},{7,1},{8,40},{9,11},... | collective-permute-start | bytes 393224 | tf_op jit(solution)/shard_map/ppermute | solution.py:48
  37.3 15.4 %collective-permute-start.6 = (bf16[4,128,512]{2,1,0:T(8,128)(2,1)S(1)}, bf16[4,128,512]{2,1,0:T(8,128)(2,1)S(1)}, u32[]{:S(2)}, u32[]{:S(2)}) collective-permute-start(bf16[4,128,512]{2,1,0:T(8,128)(2,1)S(1)} %shard_map.80.refs_0_), channel_id=1, source_target_pairs={{0,6},{1,97},{2,0},{3,99},{4,2},{5,101},{6,4},{7,103},{8,14},{9,10... | collective-permute-start | bytes 1572872 | tf_op jit(solution)/shard_map/ppermute | solution.py:48
  40.4 12.3 %collective-permute-start.7 = (bf16[4,128,512]{2,1,0:T(8,128)(2,1)S(1)}, bf16[4,128,512]{2,1,0:T(8,128)(2,1)S(1)}, u32[]{:S(2)}, u32[]{:S(2)}) collective-permute-start(bf16[4,128,512]{2,1,0:T(8,128)(2,1)S(1)} %shard_map.80.refs_0_), channel_id=1, source_target_pairs={{0,4},{1,65},{2,6},{3,67},{4,0},{5,69},{6,2},{7,71},{8,12},{9,73},... | collective-permute-start | bytes 1572872 | tf_op jit(solution)/shard_map/ppermute | solution.py:48
  41.0 15.7 %collective-permute-start.8 = (bf16[4,128,512]{2,1,0:T(8,128)(2,1)S(1)}, bf16[4,128,512]{2,1,0:T(8,128)(2,1)S(1)}, u32[]{:S(2)}, u32[]{:S(2)}) collective-permute-start(bf16[4,128,512]{2,1,0:T(8,128)(2,1)S(1)} %shard_map.80.refs_0_), channel_id=1, source_target_pairs={{0,2},{1,33},{2,4},{3,35},{4,6},{5,37},{6,0},{7,39},{8,10},{9,41},... | collective-permute-start | bytes 1572872 | tf_op jit(solution)/shard_map/ppermute | solution.py:48
  42.1 30.4 %collective-permute-start.9 = (bf16[4,128,512]{2,1,0:T(8,128)(2,1)S(1)}, bf16[4,128,512]{2,1,0:T(8,128)(2,1)S(1)}, u32[]{:S(2)}, u32[]{:S(2)}) collective-permute-start(bf16[4,128,512]{2,1,0:T(8,128)(2,1)S(1)} %shard_map.80.refs_0_), channel_id=1, source_target_pairs={{0,1},{1,0},{2,3},{3,2},{4,5},{5,4},{6,7},{7,6},{8,9},{9,8},{10,11... | collective-permute-start | bytes 1572872 | tf_op jit(solution)/shard_map/ppermute | solution.py:48
  52.7 19.8 %collective-permute-start.10 = (bf16[4,128,512]{2,1,0:T(8,128)(2,1)S(1)}, bf16[4,128,512]{2,1,0:T(8,128)(2,1)S(1)}, u32[]{:S(2)}, u32[]{:S(2)}) collective-permute-start(bf16[4,128,512]{2,1,0:T(8,128)(2,1)S(1)} %collective-permute-done.6.refs_1_), channel_id=1, source_target_pairs={{0,1},{1,0},{2,3},{3,2},{4,5},{5,4},{6,7},{7,6},{8,9},{9,8},{10,11... | collective-permute-start | bytes 1572872 | tf_op jit(solution)/shard_map/ppermute | solution.py:48
  52.7 19.8 %collective-permute-start.11 = (bf16[4,128,512]{2,1,0:T(8,128)(2,1)S(1)}, bf16[4,128,512]{2,1,0:T(8,128)(2,1)}, u32[]{:S(2)}, u32[]{:S(2)}) collective-permute-start(bf16[4,128,512]{2,1,0:T(8,128)(2,1)S(1)} %collective-permute-done.7.refs_2_), channel_id=1, source_target_pairs={{0,1},{1,0},{2,3},{3,2},{4,5},{5,4},{6,7},{7,6},{8,9},{9,8},{10,11... | collective-permute-start | bytes 1572872 | tf_op jit(solution)/shard_map/ppermute | solution.py:48
  56.7 15.9 %collective-permute-start.12 = (bf16[4,128,512]{2,1,0:T(8,128)(2,1)S(1)}, bf16[4,128,512]{2,1,0:T(8,128)(2,1)}, u32[]{:S(2)}, u32[]{:S(2)}) collective-permute-start(bf16[4,128,512]{2,1,0:T(8,128)(2,1)S(1)} %collective-permute-done.8.refs_3_), channel_id=1, source_target_pairs={{0,1},{1,0},{2,3},{3,2},{4,5},{5,4},{6,7},{7,6},{8,9},{9,8},{10,11... | collective-permute-start | bytes 1572872 | tf_op jit(solution)/shard_map/ppermute | solution.py:48
  118.3 4.2 %collective-permute-start.13 = (bf16[4,4,128,512]{3,2,1,0:T(8,128)(2,1)S(1)}, bf16[4,4,128,512]{3,2,1,0:T(8,128)(2,1)S(1)}, u32[]{:S(2)}, u32[]{:S(2)}) collective-permute-start(bf16[4,4,128,512]{3,2,1,0:T(8,128)(2,1)S(1)} %get-tuple-element.23), channel_id=1, source_target_pairs={{0,1},{1,0},{2,3},{3,2},{4,5},{5,4},{6,7},{7,6},{8,9},{9,8},{10,11... | collective-permute-start | bytes 6291464 | tf_op jit(solution)/shard_map/ppermute | solution.py:48
  125.1 36.0 %copy-start.3 = (s32[16]{0:T(128)S(1)}, s32[16]{0:T(128)}, u32[]{:S(2)}) copy-start(s32[16]{0:T(128)} %rc_ref.7) | copy-start | bytes 196
  125.1 16.1 %collective-permute-start.14 = (bf16[4,128,512]{2,1,0:T(8,128)(2,1)S(1)}, bf16[4,128,512]{2,1,0:T(8,128)(2,1)S(1)}, u32[]{:S(2)}, u32[]{:S(2)}) collective-permute-start(bf16[4,128,512]{2,1,0:T(8,128)(2,1)S(1)} %get-tuple-element.25), channel_id=1, source_target_pairs={{0,2},{1,33},{2,4},{3,35},{4,6},{5,37},{6,0},{7,39},{8,10},{9,41},... | collective-permute-start | bytes 1572872 | tf_op jit(solution)/shard_map/ppermute | solution.py:48
  125.8 15.4 %collective-permute-start.15 = (bf16[4,128,512]{2,1,0:T(8,128)(2,1)S(1)}, bf16[4,128,512]{2,1,0:T(8,128)(2,1)S(1)}, u32[]{:S(2)}, u32[]{:S(2)}) collective-permute-start(bf16[4,128,512]{2,1,0:T(8,128)(2,1)S(1)} %get-tuple-element.26), channel_id=1, source_target_pairs={{0,4},{1,65},{2,6},{3,67},{4,0},{5,69},{6,2},{7,71},{8,12},{9,73},... | collective-permute-start | bytes 1572872 | tf_op jit(solution)/shard_map/ppermute | solution.py:48
  127.8 14.3 %collective-permute-start.16 = (bf16[4,128,512]{2,1,0:T(8,128)(2,1)S(1)}, bf16[4,128,512]{2,1,0:T(8,128)(2,1)S(1)}, u32[]{:S(2)}, u32[]{:S(2)}) collective-permute-start(bf16[4,128,512]{2,1,0:T(8,128)(2,1)S(1)} %get-tuple-element.27), channel_id=1, source_target_pairs={{0,6},{1,97},{2,0},{3,99},{4,2},{5,101},{6,4},{7,103},{8,14},{9,10... | collective-permute-start | bytes 1572872 | tf_op jit(solution)/shard_map/ppermute | solution.py:48
  142.3 6.4 %collective-permute-start.19 = (f32[128,512]{1,0:T(8,128)S(1)}, f32[128,512]{1,0:T(8,128)S(1)}, u32[]{:S(2)}, u32[]{:S(2)}) collective-permute-start(f32[128,512]{1,0:T(8,128)S(1)} %get-tuple-element.31), channel_id=1, source_target_pairs={{0,96},{1,7},{2,98},{3,1},{4,100},{5,3},{6,102},{7,5},{8,104},{9,1... | collective-permute-start | bytes 786440 | tf_op jit(solution)/shard_map/ppermute | solution.py:48
  143.5 10.4 %collective-permute-start.17 = (f32[128,512]{1,0:T(8,128)S(1)}, f32[128,512]{1,0:T(8,128)S(1)}, u32[]{:S(2)}, u32[]{:S(2)}) collective-permute-start(f32[128,512]{1,0:T(8,128)S(1)} %get-tuple-element.29), channel_id=1, source_target_pairs={{0,32},{1,3},{2,34},{3,5},{4,36},{5,7},{6,38},{7,1},{8,40},{9,11},... | collective-permute-start | bytes 786440 | tf_op jit(solution)/shard_map/ppermute | solution.py:48
  144.4 9.5 %collective-permute-start.18 = (f32[128,512]{1,0:T(8,128)S(1)}, f32[128,512]{1,0:T(8,128)S(1)}, u32[]{:S(2)}, u32[]{:S(2)}) collective-permute-start(f32[128,512]{1,0:T(8,128)S(1)} %get-tuple-element.30), channel_id=1, source_target_pairs={{0,64},{1,5},{2,66},{3,7},{4,68},{5,1},{6,70},{7,3},{8,72},{9,13},... | collective-permute-start | bytes 786440 | tf_op jit(solution)/shard_map/ppermute | solution.py:48
  154.0 5.5 %collective-permute-start.20 = (f32[32,512]{1,0:T(8,128)S(1)}, f32[32,512]{1,0:T(8,128)S(1)}, u32[]{:S(2)}, u32[]{:S(2)}) collective-permute-start(f32[32,512]{1,0:T(8,128)S(1)} %get-tuple-element.33), channel_id=1, source_target_pairs={{0,8},{1,9},{2,10},{3,11},{4,12},{5,13},{6,14},{7,15},{8,16},{9,17... | collective-permute-start | bytes 196616 | tf_op jit(solution)/shard_map/ppermute | solution.py:48
  154.5 5.8 %collective-permute-start.21 = (f32[32,512]{1,0:T(8,128)S(1)}, f32[32,512]{1,0:T(8,128)S(1)}, u32[]{:S(2)}, u32[]{:S(2)}) collective-permute-start(f32[32,512]{1,0:T(8,128)S(1)} %get-tuple-element.34), channel_id=1, source_target_pairs={{0,16},{1,17},{2,18},{3,19},{4,20},{5,21},{6,22},{7,23},{8,24},{9,... | collective-permute-start | bytes 196616 | tf_op jit(solution)/shard_map/ppermute | solution.py:48
  156.6 4.5 %collective-permute-start.22 = (f32[32,512]{1,0:T(8,128)S(1)}, f32[32,512]{1,0:T(8,128)S(1)}, u32[]{:S(2)}, u32[]{:S(2)}) collective-permute-start(f32[32,512]{1,0:T(8,128)S(1)} %get-tuple-element.35), channel_id=1, source_target_pairs={{0,24},{1,25},{2,26},{3,27},{4,28},{5,29},{6,30},{7,31},{8,0},{9,1... | collective-permute-start | bytes 196616 | tf_op jit(solution)/shard_map/ppermute | solution.py:48
  (6 other events, 38.0 us)

commit v2 on v1

v2 whole, which is shorter than its diff:
```python
import functools

import jax
import jax.numpy as jnp
from jax import lax
from jax.experimental import pallas as pl
from jax.experimental.pallas import tpu as pltpu
from jax.sharding import PartitionSpec as P

freq_weight = 0.4
presence_weight = 0.8

N_DP, N_VOC = 16, 8
FEAT = 512
BF, F32, I32 = jnp.bfloat16, jnp.float32, jnp.int32
MIB = 1 << 20


def params(limit=32):
    return pltpu.CompilerParams(vmem_limit_bytes=limit * MIB)


def coords():
    dp, voc = lax.axis_index("dp"), lax.axis_index("vocab")
    return dp // 4, lax.rem(dp, 4), voc // 2, lax.rem(voc, 2)


def flat(x, z, y, c):
    return x * 32 + z * 8 + y * 2 + c


def shift_perm(axes, k):
    pairs = []
    for x in range(4):
        for z in range(4):
            for y in range(4):
                for c in range(2):
                    to = dict(x=x, z=z, y=y, c=c)
                    to[axes[c]] = (to[axes[c]] + k) % 4
                    pairs.append((flat(x, z, y, c), flat(**to)))
    return pairs


def pairing(axis, bits, cores=(0, 1)):
    pairs = []
    for x in range(4):
        for z in range(4):
            for y in range(4):
                for c in cores:
                    to = dict(x=x, z=z, y=y, c=c)
                    to[axis] ^= bits
                    pairs.append((flat(x, z, y, c), flat(**to)))
    return pairs


CORE_PERM = [(i, i ^ 1) for i in range(N_DP * N_VOC)]


def permute(v, pairs):
    return lax.ppermute(v, ("dp", "vocab"), pairs)


def iota(shape, dim):
    return lax.broadcasted_iota(I32, shape, dim)


VM = pl.BlockSpec(memory_space=pltpu.VMEM)
SM = pl.BlockSpec(memory_space=pltpu.SMEM)
HBM = pl.BlockSpec(memory_space=pltpu.HBM)


def my_start(rc_ref, dp):
    start = jnp.int32(0)
    for s in range(N_DP):
        start = start + jnp.where(s < dp, rc_ref[s], 0)
    return start


def pack_kernel(rc_any, hid_any, tok_any, seg_any, cot_any, out_ref, rc_ref, hid_ref, tok_ref, seg_ref, cot_ref, sems):
    pairs = ((rc_any, rc_ref), (hid_any, hid_ref), (tok_any, tok_ref), (seg_any, seg_ref), (cot_any, cot_ref))
    copies = [pltpu.make_async_copy(a, b, sems.at[i]) for i, (a, b) in enumerate(pairs)]
    for cp in copies:
        cp.start()
    for cp in copies:
        cp.wait()
    dp = lax.axis_index("dp")
    start, count = my_start(rc_ref, dp), rc_ref[dp]
    row, col = iota((64, 64), 0), iota((64, 64), 1)
    target = (row >> 4) * 4 + (row & 3)
    src = ((row >> 2) & 3) * N_DP + ((target - start) & 15)
    sel = (col == src) & (col < count)
    rows = jnp.dot(sel.astype(F32).astype(BF), hid_ref[...], preferred_element_type=F32).astype(BF)
    kind = iota((8, 32), 0)
    tok, cot = tok_ref[...], cot_ref[...]
    digit = jnp.where(kind == 0, tok & 255, jnp.where(kind == 1, (tok >> 8) & 255, jnp.where(kind == 2, tok >> 16, seg_ref[...])))
    high = cot.astype(BF).astype(F32)
    mid = (cot - high).astype(BF).astype(F32)
    low = cot - high - mid
    digit = jnp.where(kind < 4, digit.astype(F32), jnp.where(kind == 4, high, jnp.where(kind == 5, mid, low))).astype(BF)
    for a in range(N_DP):
        out_ref[a, 0:16, :] = rows[(a // 4) * 16:(a // 4) * 16 + 16]
        out_ref[a, 16:24, :] = jnp.zeros((8, FEAT), BF)
        out_ref[a, 16:24, 0:32] = digit


def placing(rc_ref, shape, slot_dim, per_source):
    x = lax.axis_index("dp") // 4
    k, row = iota(shape, slot_dim), iota(shape, 1 - slot_dim)
    s = k >> 4 if per_source == 16 else (k * 2731) >> 16
    u = k - s * per_source
    t, z = u >> 2, u & 3
    start = jnp.zeros(shape, I32)
    count = jnp.zeros(shape, I32)
    run = jnp.int32(0)
    for i in range(N_DP):
        start = jnp.where(s == i, run, start)
        count = jnp.where(s == i, rc_ref[i], count)
        run = run + rc_ref[i]
    a = x * 4 + z
    offset = (a - start) & 15
    base = (start + offset - a) >> 4
    sel = (u < 16) & (t * N_DP + offset < count) & (z * 32 + base + t == row)
    return sel.astype(F32).astype(BF)


def unpack_kernel(rc_ref, arr_ref, out_ref):
    sel = placing(rc_ref, (128, 384), 1, 24)
    out_ref[...] = jnp.dot(sel, arr_ref[...], preferred_element_type=F32).astype(BF)


def place_kernel(a0, a1, a2, a3, out_ref):
    x, z, y, c = coords()
    own = jnp.where(c == 0, x, y)
    for d, a in enumerate((a0, a1, a2, a3)):
        out_ref[pl.ds((own + d) & 3, 1)] = a[...][None]


def column(row):
    wide = jnp.broadcast_to(row, (128, row.shape[1]))
    return jnp.transpose(wide)[:, 0:1]


def code_kernel(cols, tok_ref, seg_ref, hit_ref, start_ref):
    dp, voc = lax.axis_index("dp"), lax.axis_index("vocab")
    tok, seg = tok_ref[...], seg_ref[...]
    tok_col = column(tok.astype(F32)).astype(I32)
    seg_col = column(seg.astype(F32)).astype(I32)
    prior = (seg_col == seg) & (iota((512, 512), 1) < iota((512, 512), 0))
    prior = prior.astype(F32).astype(BF)
    first = (dp * N_VOC + voc) * cols
    hits = (tok_col == first + iota((512, cols), 1)).astype(F32).astype(BF)
    hit_ref[...] = hits
    counts = jnp.dot(prior, hits, preferred_element_type=F32)
    start_ref[...] = -(freq_weight * counts) - presence_weight * (counts > 0).astype(F32)


def features(yy, core):
    return pl.ds(pl.multiple_of((yy * 2 + core) * FEAT, FEAT), FEAT)


def block_scores(ds, zero, one, head_ref, s_in, s_ref):
    x, z, y, c = coords()
    dims = (((1,), (1,)), ((), ()))
    if zero is not None:
        part = s_in[...]
        for d, block in zip(ds, zero):
            w = head_ref[:, features((y + d) & 3, 0)]
            part += lax.dot_general(block[...].reshape(512, FEAT), w, dims, preferred_element_type=F32)
        s_ref[...] = part
    else:
        s_ref[...] = s_in[...]
    if one is not None:
        part = None
        for q in range(4):
            rows = jnp.concatenate([block[q] for block in one], axis=0)
            v = lax.dot_general(rows, head_ref[:, features(q, 1)], dims, preferred_element_type=F32)
            part = v if part is None else part + v
        for i, d in enumerate(ds):
            s_ref[pl.ds(pl.multiple_of(((x + d) & 3) * 128, 128), 128), :] += part[i * 128:(i + 1) * 128]


def both_scores(ds, own, other, head_ref, s_in, s_ref):
    c = coords()[3]

    @pl.when(c == 0)
    def _():
        block_scores(ds, own, other, head_ref, s_in, s_ref)

    @pl.when(c == 1)
    def _():
        block_scores(ds, other, own, head_ref, s_in, s_ref)


def first_scores_kernel(own, other, head_ref, s_in, s_ref):
    both_scores((0,), (own,), (other,), head_ref, s_in, s_ref)


def own_scores_kernel(a1, a2, a3, head_ref, s_in, s_ref):
    both_scores((1, 2, 3), (a1, a2, a3), None, head_ref, s_in, s_ref)


def last_scores_kernel(a1, a2, a3, head_ref, s_in, hit_ref, s_ref, stat_ref, ss):
    both_scores((1, 2, 3), None, (a1, a2, a3), head_ref, s_in, s_ref)

    def rows(i, _):
        at = pl.ds(pl.multiple_of(i * 32, 32), 32)
        s = s_ref[at, :]
        m = jnp.max(s, axis=1, keepdims=True)
        ss[at, 0:1] = m
        ss[at, 1:2] = jnp.sum(jnp.exp(s - m), axis=1, keepdims=True)
        ss[at, 2:3] = jnp.sum(jnp.where(hit_ref[at, :].astype(F32) > 0.5, s, 0.0), axis=1, keepdims=True)
        return _

    lax.fori_loop(0, 16, rows, 0)
    flat_stats = jnp.transpose(ss[...])
    for j in range(3):
        for k in range(4):
            stat_ref[j * 4 + k:j * 4 + k + 1, :] = flat_stats[j:j + 1, k * 128:(k + 1) * 128]
    stat_ref[12:16, :] = jnp.zeros((4, 128), F32)


def merge(a, b):
    m = jnp.maximum(a[0:4, :], b[0:4, :])
    total = a[4:8, :] * jnp.exp(a[0:4, :] - m) + b[4:8, :] * jnp.exp(b[0:4, :] - m)
    return m, total, a[8:12, :] + b[8:12, :]


def merge_kernel(a_ref, b_ref, out_ref):
    out_ref[0:4, :], out_ref[4:8, :], out_ref[8:12, :] = merge(a_ref, b_ref)
    out_ref[12:16, :] = jnp.zeros((4, 128), F32)


def residual_kernel(s_ref, hit_ref, a_ref, b_ref, res_ref, lp_ref, cs, lps):
    x, z, y, c = coords()
    m, total, picked = merge(a_ref, b_ref)
    lps[0:4, :] = picked - m - jnp.log(total)
    mine = lps[pl.ds(x, 1), :]
    mine = pltpu.roll(mine, (128 - 32 * z) & 127, 1)
    lp_ref[...] = mine[:, 0:32]
    for k in range(4):
        cs[k * 128:(k + 1) * 128, 0:128] = jnp.transpose(jnp.broadcast_to(m[k:k + 1, :], (128, 128)))
        cs[k * 128:(k + 1) * 128, 128:256] = jnp.transpose(jnp.broadcast_to(total[k:k + 1, :], (128, 128)))

    def rows(i, _):
        at = pl.ds(pl.multiple_of(i * 32, 32), 32)
        p = jnp.exp(s_ref[at, :] - cs[at, 0:1]) / cs[at, 128:129]
        res_ref[at, :] = (hit_ref[at, :].astype(F32) - p).astype(BF)
        return _

    lax.fori_loop(0, 16, rows, 0)


def block_products(ds, core, res_ref, head_ref, got, outs):
    x, z, y, c = coords()

    def put(i, q, v):
        if got is not None:
            v = v + got[i][q].astype(F32)
        outs[i][q] = v.astype(outs[i].dtype)

    @pl.when(core == 0)
    def _():
        for i, d in enumerate(ds):
            v = jnp.dot(res_ref[...], head_ref[:, features((y + d) & 3, 0)], preferred_element_type=F32)
            for q in range(4):
                put(i, q, v[q * 128:(q + 1) * 128])

    @pl.when(core == 1)
    def _():
        rows = [res_ref[pl.ds(pl.multiple_of(((x + d) & 3) * 128, 128), 128), :] for d in ds]
        rows = jnp.concatenate(rows, axis=0)
        for q in range(4):
            v = jnp.dot(rows, head_ref[:, features(q, 1)], preferred_element_type=F32)
            for i in range(len(ds)):
                put(i, q, v[i * 128:(i + 1) * 128])


def send_products_kernel(ds, res_ref, head_ref, *outs):
    block_products(ds, 1 - coords()[3], res_ref, head_ref, None, outs)


def keep_products_kernel(ds, res_ref, head_ref, *refs):
    block_products(ds, coords()[3], res_ref, head_ref, refs[:len(ds)], refs[len(ds):])


def ring_sum_kernel(own_in, r1, r2, r3, own_ref, b1, b2, b3):
    x, z, y, c = coords()
    own = jnp.where(c == 0, x, y)
    for d, out in enumerate((own_ref, b1, b2, b3)):
        q = (own + d) & 3
        v = own_in[q].astype(F32) + r1[q].astype(F32) + r2[q].astype(F32) + r3[q].astype(F32)
        out[...] = v.astype(out.dtype)


def return_kernel(rc_ref, own_in, r1, r2, r3, out_ref):
    v = (own_in[...] + r1[...] + r2[...] + r3[...]).astype(BF)
    sel = placing(rc_ref, (256, 128), 0, 16)
    out_ref[...] = jnp.dot(sel, v, preferred_element_type=F32).astype(BF)


def slots_kernel(rc_ref, cot_ref, arr_ref, out_ref):
    dp = lax.axis_index("dp")
    start, count = my_start(rc_ref, dp), rc_ref[dp]
    j, k = iota((64, 256), 0), iota((64, 256), 1)
    a = (start + j) & 15
    sel = ((k >> 6) == (a >> 2)) & (((k >> 2) & 3) == (j >> 4)) & ((k & 3) == (a & 3)) & (j < count)
    v = jnp.dot(sel.astype(F32).astype(BF), arr_ref[...], preferred_element_type=F32)
    g = start + iota((64, 512), 0)
    here = iota((64, 512), 1) == (g & 15) * 32 + (g >> 4)
    cot = jnp.sum(jnp.where(here, cot_ref[...], 0.0), axis=1, keepdims=True)
    out_ref[...] = (v * cot).astype(BF)


def sds(shape, dtype):
    return jax.ShapeDtypeStruct(shape, dtype)


def call(kernel, ins, outs, in_specs=None, scratch=(), limit=16, cost=None, aliases=None):
    multi = isinstance(outs, (list, tuple))
    return pl.pallas_call(
        kernel,
        out_shape=outs,
        in_specs=in_specs or [VM] * len(ins),
        out_specs=[VM] * len(outs) if multi else VM,
        scratch_shapes=list(scratch),
        compiler_params=params(limit),
        cost_estimate=cost,
        input_output_aliases=aliases or {},
    )(*ins)


def cost(flops, nbytes):
    return pl.CostEstimate(flops=flops, bytes_accessed=nbytes, transcendentals=0)


def per_device(hidden, head, row_counts, token_ids, segment_ids, cotangent):
    cols = head.shape[1]
    head = head.T
    outgoing = call(
        pack_kernel,
        (row_counts, hidden, token_ids.reshape(1, 32), segment_ids.reshape(1, 32), cotangent.reshape(1, 32)),
        sds((N_DP, 24, FEAT), BF),
        in_specs=[HBM] * 5,
        scratch=[
            pltpu.SMEM((16,), I32),
            pltpu.VMEM((64, FEAT), BF),
            pltpu.VMEM((1, 32), I32),
            pltpu.VMEM((1, 32), I32),
            pltpu.VMEM((1, 32), F32),
            pltpu.SemaphoreType.DMA((5,)),
        ],
    )
    arrived = lax.all_to_all(outgoing, "dp", 0, 0, tiled=True)
    g1 = call(unpack_kernel, (row_counts, arrived.reshape(384, FEAT)), sds((128, FEAT), BF), in_specs=[SM, VM])
    digits = arrived[:, 16:24, 0:32].astype(F32)
    tokens = (digits[:, 0] + 256.0 * digits[:, 1] + 65536.0 * digits[:, 2]).astype(I32).reshape(1, 512)
    segments = digits[:, 3].astype(I32).reshape(1, 512)
    cots = (digits[:, 4] + digits[:, 5] + digits[:, 6]).reshape(1, 512)

    second = [g1] + [permute(g1, shift_perm("xy", 4 - d)) for d in (1, 2, 3)]
    hits, s = call(
        functools.partial(code_kernel, cols),
        (tokens, segments),
        [sds((512, cols), BF), sds((512, cols), F32)],
        cost=cost(1 << 20, 1 << 10),
    )
    second, s = lax.optimization_barrier((second, s))
    g2 = call(place_kernel, second, sds((4, 128, FEAT), BF))
    third = [g2] + [permute(g2, shift_perm("yx", 4 - d)) for d in (1, 2, 3)]

    wide = sds((512, cols), F32)
    small = cost(1 << 20, 1 << 10)
    other = permute(g2, CORE_PERM)
    s = call(first_scores_kernel, (g2, other, head, s), wide, cost=small, aliases={3: 0})
    *third, s = lax.optimization_barrier((*third[1:], s))
    other = [permute(v, CORE_PERM) for v in third]
    s = call(own_scores_kernel, (*third, head, s), wide, cost=small, aliases={4: 0})
    s, stats = call(
        last_scores_kernel,
        (*other, head, s, hits),
        [wide, sds((16, 128), F32)],
        scratch=[pltpu.VMEM((512, 128), F32)],
        aliases={4: 0},
    )
    steps = [CORE_PERM] + [pairing(ax, b) for ax in "yxz" for b in (1, 3)]
    for i, pairs in enumerate(steps):
        got_stats = permute(stats, pairs)
        if i < 6:
            stats = call(merge_kernel, (stats, got_stats), sds((16, 128), F32))

    res, logprobs = call(
        residual_kernel,
        (s, hits, stats, got_stats),
        [sds((512, cols), BF), sds((1, 32), F32)],
        scratch=[pltpu.VMEM((512, 256), F32), pltpu.VMEM((8, 128), F32)],
    )
    quarter = sds((4, 128, FEAT), BF)
    got, ring = {}, {}
    pairs = ((1, 3), (2, 0))
    for ds in pairs:
        out = call(functools.partial(send_products_kernel, ds), (res, head), [quarter] * 2, cost=small)
        for d, v in zip(ds, out):
            got[d] = permute(v, CORE_PERM)
        res, _ = lax.optimization_barrier((res, out[0]))
    for ds in pairs:
        out = [quarter if d else sds((4, 128, FEAT), F32) for d in ds]
        out = call(functools.partial(keep_products_kernel, ds), (res, head, *[got[d] for d in ds]), out, cost=small)
        for d, v in zip(ds, out):
            ring[d] = permute(v, shift_perm("yx", d)) if d else v
        res, _ = lax.optimization_barrier((res, out[0]))
    own, *out = call(ring_sum_kernel, [ring[d] for d in range(4)], [sds((128, FEAT), F32)] * 4)
    ring = [permute(v, shift_perm("xy", d + 1)) for d, v in enumerate(out)]
    returning = call(
        return_kernel, (row_counts, own, *ring), sds((256, FEAT), BF), in_specs=[SM] + [VM] * 4
    )
    returned = lax.all_to_all(returning.reshape(N_DP, 16, FEAT), "dp", 0, 0, tiled=True)
    grad_hidden = call(
        slots_kernel, (row_counts, cots, returned.reshape(256, FEAT)), sds((64, FEAT), BF), in_specs=[SM, VM, VM]
    )
    return logprobs.reshape(32), grad_hidden


def solution(mesh):
    return jax.shard_map(
        per_device,
        mesh=mesh,
        in_specs=(P("dp", "vocab"), P(None, ("dp", "vocab")), P(), P("dp"), P("dp"), P("dp")),
        out_specs=(P("dp"), P("dp", "vocab")),
        check_vma=False,
    )
```

time: 176 us -> 139 us (0.79)
  blocking collectives: 46.7 us -> 17.7 us
  local copies, waits for them, and re-layouts: 19.4 us -> 7.49 us
  starting transfers between devices: 22.3 us -> 33.8 us
  Pallas kernels: 32.5 us -> 26.3 us
    all_to_all x4 -> x1, blocking collectives: 46.7 us -> 17.7 us  [per_device(): arrived = lax.all_to_all(outgoing, 'dp', 0, 0, tiled=True)]
    unnamed x15 -> x20, local copies, waits for them, and re-layouts: 19.2 us -> 7.25 us
    ppermute x23 -> x27, waiting for transfers between devices: 53.8 us -> 44.1 us  [permute(): return lax.ppermute(v, ('dp', 'vocab'), pairs)]
    all_to_all x0 -> x1, waiting for transfers between devices: none -> 8.34 us  [per_device(): lax.all_to_all(returning.reshape(N_DP, 16, FEAT), 'dp', 0, 0, tiled=True)]
    ppermute x23 -> x27, starting transfers between devices: 22.3 us -> 29.4 us  [permute(): return lax.ppermute(v, ('dp', 'vocab'), pairs)]
    pallas_call x13 -> x21, Pallas kernels: 32.5 us -> 26.3 us  [call(): pl.pallas_call(kernel, out_shape=outs, in_specs=in_specs or [VM] * len(in...]
    all_to_all x0 -> x1, starting transfers between devices: none -> 4.38 us  [per_device(): lax.all_to_all(returning.reshape(N_DP, 16, FEAT), 'dp', 0, 0, tiled=True)]
  transfers between devices with their start and end apart: 23 -> 28, of which waited for: 16 -> 15; matrix products, arithmetic and copies ran while one was open for 8% -> 0% of each run, Pallas kernels for 1% -> 8%
where the time goes in v2:
time: 139 us
  waiting for transfers between devices  52.4 us (38%)
  starting transfers between devices  33.8 us (24%)
  Pallas kernels  26.3 us (19%)
  blocking collectives  17.7 us (13%)
  local copies, waits for them, and re-layouts  7.49 us (5%)
    ppermute x27, waiting for transfers between devices, permute(): return lax.ppermute(v, ('dp', 'vocab'), pairs)  44.1 us
    ppermute x27, starting transfers between devices, permute(): return lax.ppermute(v, ('dp', 'vocab'), pairs)  29.4 us
    pallas_call x21, Pallas kernels, call(): pl.pallas_call(kernel, out_shape=outs, in_specs=in_specs or [VM] * len(in...  26.3 us
    all_to_all x1, blocking collectives, per_device(): arrived = lax.all_to_all(outgoing, 'dp', 0, 0, tiled=True)  17.7 us
    all_to_all x1, waiting for transfers between devices, per_device(): lax.all_to_all(returning.reshape(N_DP, 16, FEAT), 'dp', 0, 0, tiled=True)  8.34 us
    unnamed x20, local copies, waits for them, and re-layouts  7.25 us
    all_to_all x1, starting transfers between devices, per_device(): lax.all_to_all(returning.reshape(N_DP, 16, FEAT), 'dp', 0, 0, tiled=True)  4.38 us
  transfers between devices with their start and end apart: 28, of which 15 were waited for; matrix products, arithmetic and copies ran while one was open for 0% of the time, Pallas kernels for 8%

profile of v2, /device:TPU:0, one launch (start us, length us, event | category | flops | bytes accessed | tf_op | source)
XLA Modules:
  0.0 138.6 jit_solution(9546826808816770062)
XLA Ops:
  4.9 17.7 %all_to_all.10 = bf16[16,24,512]{2,1,0:T(8,128)(2,1)S(1)} all-to-all(bf16[16,24,512]{2,1,0:T(8,128)(2,1)S(1)} %shard_map.77), channel_id=1, replica_groups=mesh['dp'=16,'vocab'=8] {'dp'}, dimensions={0} | all-to-all | bytes 786432 | tf_op jit(solution)/shard_map/all_to_all | solution.py:353
  23.5 2.7 %collective-permute-start.1 = (bf16[128,512]{1,0:T(8,128)(2,1)S(1)}, bf16[128,512]{1,0:T(8,128)(2,1)S(1)}, u32[]{:S(2)}, u32[]{:S(2)}) collective-permute-start(bf16[128,512]{1,0:T(8,128)(2,1)S(1)} %shard_map.78.a0), channel_id=1, source_target_pairs={{0,64},{1,5},{2,66},{3,7},{4,68},{5,1},{6,70},{7,3},{8,72},{9,13},... | collective-permute-start | bytes 393224 | tf_op jit(solution)/shard_map/ppermute | solution.py:60
  33.7 2.9 %collective-permute-start.4 = (bf16[4,128,512]{2,1,0:T(8,128)(2,1)S(1)}, bf16[4,128,512]{2,1,0:T(8,128)(2,1)S(1)}, u32[]{:S(2)}, u32[]{:S(2)}) collective-permute-start(bf16[4,128,512]{2,1,0:T(8,128)(2,1)S(1)} %shard_map.80.own), channel_id=1, source_target_pairs={{0,4},{1,65},{2,6},{3,67},{4,0},{5,69},{6,2},{7,71},{8,12},{9,73},... | collective-permute-start | bytes 1572872 | tf_op jit(solution)/shard_map/ppermute | solution.py:60
  37.9 3.8 %copy-done = bf16[4096,1187]{0,1:T(8,128)(2,1)S(1)} copy-done((bf16[4096,1187]{0,1:T(8,128)(2,1)S(1)}, bf16[4096,1187]{0,1:T(8,128)(2,1)}, u32[]{:S(2)}) %copy-start) | copy-done | bytes 9723928
  41.7 2.4 %shard_map.81.s_in = f32[512,1187]{1,0:T(8,128)S(1)} custom-call(bf16[4,128,512]{2,1,0:T(8,128)(2,1)S(1)} %shard_map.80.own, bf16[4,128,512]{2,1,0:T(8,128)(2,1)S(1)} %collective-permute-done.6.other, bf16[1187,4096]{1,0:T(8,128)(2,1)S(1)} %bitcast.8, f32[512,1187]{1,0:T(8,128)S(1)} %get-tuple-element.37.s_in), custom_call_target="tpu_custom_call", output_to_operand_aliasing={{}: (3, {})} | custom-call | flops 1048576 | bytes 1024 | tf_op jit(solution)/shard_map/pallas_call | solution.py:320
  44.1 5.2 %collective-permute-done.4.a2 = bf16[4,128,512]{2,1,0:T(8,128)(2,1)S(1)} collective-permute-done((bf16[4,128,512]{2,1,0:T(8,128)(2,1)S(1)}, bf16[4,128,512]{2,1,0:T(8,128)(2,1)S(1)}, u32[]{:S(2)}, u32[]{:S(2)}) %collective-permute-start.4) | collective-permute-done | bytes 524320 | tf_op jit(solution)/shard_map/ppermute | solution.py:60
  49.9 2.8 %shard_map.82.s_in = f32[512,1187]{1,0:T(8,128)S(1)} custom-call(bf16[4,128,512]{2,1,0:T(8,128)(2,1)S(1)} %collective-permute-done.3.a1, bf16[4,128,512]{2,1,0:T(8,128)(2,1)S(1)} %collective-permute-done.4.a2, bf16[4,128,512]{2,1,0:T(8,128)(2,1)S(1)} %collective-permute-done.5.a3, bf16[1187,4096]{1,0:T(8,128)(2,1)S(1)} %bitcast.11, ...), custom_call_target="tpu_custom_call", output_to_operand_aliasing={{}: (4, {})} | custom-call | flops 1048576 | bytes 1024 | tf_op jit(solution)/shard_map/pallas_call | solution.py:320
  52.8 6.0 %shard_map.83 = (f32[512,1187]{1,0:T(8,128)S(1)}, f32[16,128]{1,0:T(8,128)S(1)}) custom-call(bf16[4,128,512]{2,1,0:T(8,128)(2,1)S(1)} %collective-permute-done.7.a1, bf16[4,128,512]{2,1,0:T(8,128)(2,1)S(1)} %collective-permute-done.8.a2, bf16[4,128,512]{2,1,0:T(8,128)(2,1)S(1)} %collective-permute-done.9.a3, ...), custom_call_target="tpu_custom_call", output_to_operand_aliasing={{0}: (4, {})} | custom-call | tf_op jit(solution)/shard_map/pallas_call | solution.py:320
  61.9 2.0 %collective-permute-done.11.b_ref = f32[16,128]{1,0:T(8,128)S(1)} collective-permute-done((f32[16,128]{1,0:T(8,128)S(1)}, f32[16,128]{1,0:T(8,128)S(1)}, u32[]{:S(2)}, u32[]{:S(2)}) %collective-permute-start.11) | collective-permute-done | bytes 8224 | tf_op jit(solution)/shard_map/ppermute | solution.py:60
  63.9 2.4 %collective-permute-start.12 = (f32[16,128]{1,0:T(8,128)S(1)}, f32[16,128]{1,0:T(8,128)S(1)}, u32[]{:S(2)}, u32[]{:S(2)}) collective-permute-start(f32[16,128]{1,0:T(8,128)S(1)} %shard_map.85.a_ref), channel_id=1, source_target_pairs={{0,6},{1,7},{2,4},{3,5},{4,2},{5,3},{6,0},{7,1},{8,14},{9,15},{10,... | collective-permute-start | bytes 24584 | tf_op jit(solution)/shard_map/ppermute | solution.py:60
  66.3 2.6 %collective-permute-done.12.b_ref = f32[16,128]{1,0:T(8,128)S(1)} collective-permute-done((f32[16,128]{1,0:T(8,128)S(1)}, f32[16,128]{1,0:T(8,128)S(1)}, u32[]{:S(2)}, u32[]{:S(2)}) %collective-permute-start.12) | collective-permute-done | bytes 8224 | tf_op jit(solution)/shard_map/ppermute | solution.py:60
  69.7 2.9 %collective-permute-done.13.b_ref = f32[16,128]{1,0:T(8,128)S(1)} collective-permute-done((f32[16,128]{1,0:T(8,128)S(1)}, f32[16,128]{1,0:T(8,128)S(1)}, u32[]{:S(2)}, u32[]{:S(2)}) %collective-permute-start.13) | collective-permute-done | bytes 8224 | tf_op jit(solution)/shard_map/ppermute | solution.py:60
  72.6 2.8 %collective-permute-start.14 = (f32[16,128]{1,0:T(8,128)S(1)}, f32[16,128]{1,0:T(8,128)S(1)}, u32[]{:S(2)}, u32[]{:S(2)}) collective-permute-start(f32[16,128]{1,0:T(8,128)S(1)} %shard_map.87.a_ref), channel_id=1, source_target_pairs={{0,96},{1,97},{2,98},{3,99},{4,100},{5,101},{6,102},{7,103},{8,104... | collective-permute-start | bytes 24584 | tf_op jit(solution)/shard_map/ppermute | solution.py:60
  75.4 2.2 %collective-permute-done.14.b_ref = f32[16,128]{1,0:T(8,128)S(1)} collective-permute-done((f32[16,128]{1,0:T(8,128)S(1)}, f32[16,128]{1,0:T(8,128)S(1)}, u32[]{:S(2)}, u32[]{:S(2)}) %collective-permute-start.14) | collective-permute-done | bytes 8224 | tf_op jit(solution)/shard_map/ppermute | solution.py:60
  77.9 3.4 %collective-permute-done.15.b_ref = f32[16,128]{1,0:T(8,128)S(1)} collective-permute-done((f32[16,128]{1,0:T(8,128)S(1)}, f32[16,128]{1,0:T(8,128)S(1)}, u32[]{:S(2)}, u32[]{:S(2)}) %collective-permute-start.15) | collective-permute-done | bytes 8224 | tf_op jit(solution)/shard_map/ppermute | solution.py:60
  82.3 3.9 %collective-permute-done.16.b_ref = f32[16,128]{1,0:T(8,128)S(1)} collective-permute-done((f32[16,128]{1,0:T(8,128)S(1)}, f32[16,128]{1,0:T(8,128)S(1)}, u32[]{:S(2)}, u32[]{:S(2)}) %collective-permute-start.16) | collective-permute-done | bytes 8224 | tf_op jit(solution)/shard_map/ppermute | solution.py:60
  86.2 2.5 %shard_map.90 = (bf16[512,1187]{1,0:T(8,128)(2,1)S(1)}, f32[1,32]{1,0:T(1,128)}) custom-call(f32[512,1187]{1,0:T(8,128)S(1)} %get-tuple-element.43.s_ref, bf16[512,1187]{1,0:T(8,128)(2,1)S(1)} %get-tuple-element.42.hit_ref, f32[16,128]{1,0:T(8,128)S(1)} %shard_map.89.a_ref, f32[16,128]{1,0:T(8,128)S(1)} %collective-permute-done.16.b_ref), custom_call_target="tpu_custom_call" | custom-call | tf_op jit(solution)/shard_map/pallas_call | solution.py:320
  95.0 2.8 %collective-permute-start.23 = (bf16[4,128,512]{2,1,0:T(8,128)(2,1)S(1)}, bf16[4,128,512]{2,1,0:T(8,128)(2,1)S(1)}, u32[]{:S(2)}, u32[]{:S(2)}) collective-permute-start(bf16[4,128,512]{2,1,0:T(8,128)(2,1)S(1)} %get-tuple-element.57), channel_id=1, source_target_pairs={{0,6},{1,97},{2,0},{3,99},{4,2},{5,101},{6,4},{7,103},{8,14},{9,10... | collective-permute-start | bytes 1572872 | tf_op jit(solution)/shard_map/ppermute | solution.py:60
  100.0 10.1 %collective-permute-done.23.r3 = bf16[4,128,512]{2,1,0:T(8,128)(2,1)S(1)} collective-permute-done((bf16[4,128,512]{2,1,0:T(8,128)(2,1)S(1)}, bf16[4,128,512]{2,1,0:T(8,128)(2,1)S(1)}, u32[]{:S(2)}, u32[]{:S(2)}) %collective-permute-start.23) | collective-permute-done | bytes 524320 | tf_op jit(solution)/shard_map/ppermute | solution.py:60
  111.4 4.1 %collective-permute-start.25 = (f32[128,512]{1,0:T(8,128)S(1)}, f32[128,512]{1,0:T(8,128)S(1)}, u32[]{:S(2)}, u32[]{:S(2)}) collective-permute-start(f32[128,512]{1,0:T(8,128)S(1)} %get-tuple-element.60), channel_id=1, source_target_pairs={{0,64},{1,5},{2,66},{3,7},{4,68},{5,1},{6,70},{7,3},{8,72},{9,13},... | collective-permute-start | bytes 786440 | tf_op jit(solution)/shard_map/ppermute | solution.py:60
  115.6 3.4 %collective-permute-done.24.r1 = f32[128,512]{1,0:T(8,128)S(1)} collective-permute-done((f32[128,512]{1,0:T(8,128)S(1)}, f32[128,512]{1,0:T(8,128)S(1)}, u32[]{:S(2)}, u32[]{:S(2)}) %collective-permute-start.24) | collective-permute-done | bytes 262176 | tf_op jit(solution)/shard_map/ppermute | solution.py:60
  119.0 3.7 %collective-permute-done.25.r2 = f32[128,512]{1,0:T(8,128)S(1)} collective-permute-done((f32[128,512]{1,0:T(8,128)S(1)}, f32[128,512]{1,0:T(8,128)S(1)}, u32[]{:S(2)}, u32[]{:S(2)}) %collective-permute-start.25) | collective-permute-done | bytes 262176 | tf_op jit(solution)/shard_map/ppermute | solution.py:60
  124.4 4.4 %all-to-all-start.1 = ((bf16[16,16,512]{2,1,0:T(8,128)(2,1)}), bf16[16,16,512]{2,1,0:T(8,128)(2,1)S(1)}, u32[]{:S(2)}, u32[]{:S(2)}) async-start(bf16[16,16,512]{2,1,0:T(8,128)(2,1)} %bitcast.6), calls=%async_computation.1 | async-start | bytes 524288 | tf_op jit(solution)/shard_map/all_to_all | solution.py:416
  128.9 8.3 %all-to-all-done.1 = bf16[16,16,512]{2,1,0:T(8,128)(2,1)S(1)} async-done(((bf16[16,16,512]{2,1,0:T(8,128)(2,1)}), bf16[16,16,512]{2,1,0:T(8,128)(2,1)S(1)}, u32[]{:S(2)}, u32[]{:S(2)}) %all-to-all-start.1) | async-done | bytes 262176 | tf_op jit(solution)/shard_map/all_to_all | solution.py:416
  (81 shorter events, 32.6 us)
Async XLA Ops:
  23.4 7.7 %collective-permute-start.2 = (bf16[128,512]{1,0:T(8,128)(2,1)S(1)}, bf16[128,512]{1,0:T(8,128)(2,1)S(1)}, u32[]{:S(2)}, u32[]{:S(2)}) collective-permute-start(bf16[128,512]{1,0:T(8,128)(2,1)S(1)} %shard_map.78.a0), channel_id=1, source_target_pairs={{0,32},{1,3},{2,34},{3,5},{4,36},{5,7},{6,38},{7,1},{8,40},{9,11},... | collective-permute-start | bytes 393224 | tf_op jit(solution)/shard_map/ppermute | solution.py:60
  23.5 7.5 %collective-permute-start.1 = (bf16[128,512]{1,0:T(8,128)(2,1)S(1)}, bf16[128,512]{1,0:T(8,128)(2,1)S(1)}, u32[]{:S(2)}, u32[]{:S(2)}) collective-permute-start(bf16[128,512]{1,0:T(8,128)(2,1)S(1)} %shard_map.78.a0), channel_id=1, source_target_pairs={{0,64},{1,5},{2,66},{3,7},{4,68},{5,1},{6,70},{7,3},{8,72},{9,13},... | collective-permute-start | bytes 393224 | tf_op jit(solution)/shard_map/ppermute | solution.py:60
  26.2 5.7 %collective-permute-start = (bf16[128,512]{1,0:T(8,128)(2,1)S(1)}, bf16[128,512]{1,0:T(8,128)(2,1)S(1)}, u32[]{:S(2)}, u32[]{:S(2)}) collective-permute-start(bf16[128,512]{1,0:T(8,128)(2,1)S(1)} %shard_map.78.a0), channel_id=1, source_target_pairs={{0,96},{1,7},{2,98},{3,1},{4,100},{5,3},{6,102},{7,5},{8,104},{9,1... | collective-permute-start | bytes 393224 | tf_op jit(solution)/shard_map/ppermute | solution.py:60
  31.9 6.0 %collective-permute-start.6 = (bf16[4,128,512]{2,1,0:T(8,128)(2,1)S(1)}, bf16[4,128,512]{2,1,0:T(8,128)(2,1)S(1)}, u32[]{:S(2)}, u32[]{:S(2)}) collective-permute-start(bf16[4,128,512]{2,1,0:T(8,128)(2,1)S(1)} %shard_map.80.own), channel_id=1, source_target_pairs={{0,1},{1,0},{2,3},{3,2},{4,5},{5,4},{6,7},{7,6},{8,9},{9,8},{10,11... | collective-permute-start | bytes 1572872 | tf_op jit(solution)/shard_map/ppermute | solution.py:60
  32.0 12.1 %collective-permute-start.5 = (bf16[4,128,512]{2,1,0:T(8,128)(2,1)S(1)}, bf16[4,128,512]{2,1,0:T(8,128)(2,1)S(1)}, u32[]{:S(2)}, u32[]{:S(2)}) collective-permute-start(bf16[4,128,512]{2,1,0:T(8,128)(2,1)S(1)} %shard_map.80.own), channel_id=1, source_target_pairs={{0,2},{1,33},{2,4},{3,35},{4,6},{5,37},{6,0},{7,39},{8,10},{9,41},... | collective-permute-start | bytes 1572872 | tf_op jit(solution)/shard_map/ppermute | solution.py:60
  33.7 15.7 %collective-permute-start.4 = (bf16[4,128,512]{2,1,0:T(8,128)(2,1)S(1)}, bf16[4,128,512]{2,1,0:T(8,128)(2,1)S(1)}, u32[]{:S(2)}, u32[]{:S(2)}) collective-permute-start(bf16[4,128,512]{2,1,0:T(8,128)(2,1)S(1)} %shard_map.80.own), channel_id=1, source_target_pairs={{0,4},{1,65},{2,6},{3,67},{4,0},{5,69},{6,2},{7,71},{8,12},{9,73},... | collective-permute-start | bytes 1572872 | tf_op jit(solution)/shard_map/ppermute | solution.py:60
  36.6 12.8 %collective-permute-start.3 = (bf16[4,128,512]{2,1,0:T(8,128)(2,1)S(1)}, bf16[4,128,512]{2,1,0:T(8,128)(2,1)S(1)}, u32[]{:S(2)}, u32[]{:S(2)}) collective-permute-start(bf16[4,128,512]{2,1,0:T(8,128)(2,1)S(1)} %shard_map.80.own), channel_id=1, source_target_pairs={{0,6},{1,97},{2,0},{3,99},{4,2},{5,101},{6,4},{7,103},{8,14},{9,10... | collective-permute-start | bytes 1572872 | tf_op jit(solution)/shard_map/ppermute | solution.py:60
  49.4 3.4 %collective-permute-start.7 = (bf16[4,128,512]{2,1,0:T(8,128)(2,1)S(1)}, bf16[4,128,512]{2,1,0:T(8,128)(2,1)S(1)}, u32[]{:S(2)}, u32[]{:S(2)}) collective-permute-start(bf16[4,128,512]{2,1,0:T(8,128)(2,1)S(1)} %collective-permute-done.3.a1), channel_id=1, source_target_pairs={{0,1},{1,0},{2,3},{3,2},{4,5},{5,4},{6,7},{7,6},{8,9},{9,8},{10,11... | collective-permute-start | bytes 1572872 | tf_op jit(solution)/shard_map/ppermute | solution.py:60
  49.4 3.4 %collective-permute-start.8 = (bf16[4,128,512]{2,1,0:T(8,128)(2,1)S(1)}, bf16[4,128,512]{2,1,0:T(8,128)(2,1)S(1)}, u32[]{:S(2)}, u32[]{:S(2)}) collective-permute-start(bf16[4,128,512]{2,1,0:T(8,128)(2,1)S(1)} %collective-permute-done.4.a2), channel_id=1, source_target_pairs={{0,1},{1,0},{2,3},{3,2},{4,5},{5,4},{6,7},{7,6},{8,9},{9,8},{10,11... | collective-permute-start | bytes 1572872 | tf_op jit(solution)/shard_map/ppermute | solution.py:60
  60.2 3.7 %collective-permute-start.11 = (f32[16,128]{1,0:T(8,128)S(1)}, f32[16,128]{1,0:T(8,128)S(1)}, u32[]{:S(2)}, u32[]{:S(2)}) collective-permute-start(f32[16,128]{1,0:T(8,128)S(1)} %shard_map.84.a_ref), channel_id=1, source_target_pairs={{0,2},{1,3},{2,0},{3,1},{4,6},{5,7},{6,4},{7,5},{8,10},{9,11},{10,... | collective-permute-start | bytes 24584 | tf_op jit(solution)/shard_map/ppermute | solution.py:60
  63.9 4.9 %collective-permute-start.12 = (f32[16,128]{1,0:T(8,128)S(1)}, f32[16,128]{1,0:T(8,128)S(1)}, u32[]{:S(2)}, u32[]{:S(2)}) collective-permute-start(f32[16,128]{1,0:T(8,128)S(1)} %shard_map.85.a_ref), channel_id=1, source_target_pairs={{0,6},{1,7},{2,4},{3,5},{4,2},{5,3},{6,0},{7,1},{8,14},{9,15},{10,... | collective-permute-start | bytes 24584 | tf_op jit(solution)/shard_map/ppermute | solution.py:60
  68.9 3.7 %collective-permute-start.13 = (f32[16,128]{1,0:T(8,128)S(1)}, f32[16,128]{1,0:T(8,128)S(1)}, u32[]{:S(2)}, u32[]{:S(2)}) collective-permute-start(f32[16,128]{1,0:T(8,128)S(1)} %shard_map.86.a_ref), channel_id=1, source_target_pairs={{0,32},{1,33},{2,34},{3,35},{4,36},{5,37},{6,38},{7,39},{8,40},{9,... | collective-permute-start | bytes 24584 | tf_op jit(solution)/shard_map/ppermute | solution.py:60
  72.6 4.9 %collective-permute-start.14 = (f32[16,128]{1,0:T(8,128)S(1)}, f32[16,128]{1,0:T(8,128)S(1)}, u32[]{:S(2)}, u32[]{:S(2)}) collective-permute-start(f32[16,128]{1,0:T(8,128)S(1)} %shard_map.87.a_ref), channel_id=1, source_target_pairs={{0,96},{1,97},{2,98},{3,99},{4,100},{5,101},{6,102},{7,103},{8,104... | collective-permute-start | bytes 24584 | tf_op jit(solution)/shard_map/ppermute | solution.py:60
  77.6 3.7 %collective-permute-start.15 = (f32[16,128]{1,0:T(8,128)S(1)}, f32[16,128]{1,0:T(8,128)S(1)}, u32[]{:S(2)}, u32[]{:S(2)}) collective-permute-start(f32[16,128]{1,0:T(8,128)S(1)} %shard_map.88.a_ref), channel_id=1, source_target_pairs={{0,8},{1,9},{2,10},{3,11},{4,12},{5,13},{6,14},{7,15},{8,0},{9,1},... | collective-permute-start | bytes 24584 | tf_op jit(solution)/shard_map/ppermute | solution.py:60
  81.3 4.9 %collective-permute-start.16 = (f32[16,128]{1,0:T(8,128)S(1)}, f32[16,128]{1,0:T(8,128)S(1)}, u32[]{:S(2)}, u32[]{:S(2)}) collective-permute-start(f32[16,128]{1,0:T(8,128)S(1)} %shard_map.89.a_ref), channel_id=1, source_target_pairs={{0,24},{1,25},{2,26},{3,27},{4,28},{5,29},{6,30},{7,31},{8,16},{9,... | collective-permute-start | bytes 24584 | tf_op jit(solution)/shard_map/ppermute | solution.py:60
  92.4 5.5 %collective-permute-start.20 = (bf16[4,128,512]{2,1,0:T(8,128)(2,1)S(1)}, bf16[4,128,512]{2,1,0:T(8,128)(2,1)S(1)}, u32[]{:S(2)}, u32[]{:S(2)}) collective-permute-start(bf16[4,128,512]{2,1,0:T(8,128)(2,1)S(1)} %get-tuple-element.54), channel_id=1, source_target_pairs={{0,1},{1,0},{2,3},{3,2},{4,5},{5,4},{6,7},{7,6},{8,9},{9,8},{10,11... | collective-permute-start | bytes 1572872 | tf_op jit(solution)/shard_map/ppermute | solution.py:60
  92.6 5.3 %collective-permute-start.19 = (bf16[4,128,512]{2,1,0:T(8,128)(2,1)S(1)}, bf16[4,128,512]{2,1,0:T(8,128)(2,1)S(1)}, u32[]{:S(2)}, u32[]{:S(2)}) collective-permute-start(bf16[4,128,512]{2,1,0:T(8,128)(2,1)S(1)} %get-tuple-element.49), channel_id=1, source_target_pairs={{0,1},{1,0},{2,3},{3,2},{4,5},{5,4},{6,7},{7,6},{8,9},{9,8},{10,11... | collective-permute-start | bytes 1572872 | tf_op jit(solution)/shard_map/ppermute | solution.py:60
  94.6 15.6 %collective-permute-start.21 = (bf16[4,128,512]{2,1,0:T(8,128)(2,1)S(1)}, bf16[4,128,512]{2,1,0:T(8,128)(2,1)S(1)}, u32[]{:S(2)}, u32[]{:S(2)}) collective-permute-start(bf16[4,128,512]{2,1,0:T(8,128)(2,1)S(1)} %get-tuple-element.52), channel_id=1, source_target_pairs={{0,2},{1,33},{2,4},{3,35},{4,6},{5,37},{6,0},{7,39},{8,10},{9,41},... | collective-permute-start | bytes 1572872 | tf_op jit(solution)/shard_map/ppermute | solution.py:60
  95.0 15.1 %collective-permute-start.23 = (bf16[4,128,512]{2,1,0:T(8,128)(2,1)S(1)}, bf16[4,128,512]{2,1,0:T(8,128)(2,1)S(1)}, u32[]{:S(2)}, u32[]{:S(2)}) collective-permute-start(bf16[4,128,512]{2,1,0:T(8,128)(2,1)S(1)} %get-tuple-element.57), channel_id=1, source_target_pairs={{0,6},{1,97},{2,0},{3,99},{4,2},{5,101},{6,4},{7,103},{8,14},{9,10... | collective-permute-start | bytes 1572872 | tf_op jit(solution)/shard_map/ppermute | solution.py:60
  99.4 11.7 %collective-permute-start.22 = (bf16[4,128,512]{2,1,0:T(8,128)(2,1)S(1)}, bf16[4,128,512]{2,1,0:T(8,128)(2,1)S(1)}, u32[]{:S(2)}, u32[]{:S(2)}) collective-permute-start(bf16[4,128,512]{2,1,0:T(8,128)(2,1)S(1)} %get-tuple-element.56), channel_id=1, source_target_pairs={{0,4},{1,65},{2,6},{3,67},{4,0},{5,69},{6,2},{7,71},{8,12},{9,73},... | collective-permute-start | bytes 1572872 | tf_op jit(solution)/shard_map/ppermute | solution.py:60
  111.4 7.7 %collective-permute-start.24 = (f32[128,512]{1,0:T(8,128)S(1)}, f32[128,512]{1,0:T(8,128)S(1)}, u32[]{:S(2)}, u32[]{:S(2)}) collective-permute-start(f32[128,512]{1,0:T(8,128)S(1)} %get-tuple-element.59), channel_id=1, source_target_pairs={{0,32},{1,3},{2,34},{3,5},{4,36},{5,7},{6,38},{7,1},{8,40},{9,11},... | collective-permute-start | bytes 786440 | tf_op jit(solution)/shard_map/ppermute | solution.py:60
  111.4 11.3 %collective-permute-start.25 = (f32[128,512]{1,0:T(8,128)S(1)}, f32[128,512]{1,0:T(8,128)S(1)}, u32[]{:S(2)}, u32[]{:S(2)}) collective-permute-start(f32[128,512]{1,0:T(8,128)S(1)} %get-tuple-element.60), channel_id=1, source_target_pairs={{0,64},{1,5},{2,66},{3,7},{4,68},{5,1},{6,70},{7,3},{8,72},{9,13},... | collective-permute-start | bytes 786440 | tf_op jit(solution)/shard_map/ppermute | solution.py:60
  115.6 7.2 %collective-permute-start.26 = (f32[128,512]{1,0:T(8,128)S(1)}, f32[128,512]{1,0:T(8,128)S(1)}, u32[]{:S(2)}, u32[]{:S(2)}) collective-permute-start(f32[128,512]{1,0:T(8,128)S(1)} %get-tuple-element.61), channel_id=1, source_target_pairs={{0,96},{1,7},{2,98},{3,1},{4,100},{5,3},{6,102},{7,5},{8,104},{9,1... | collective-permute-start | bytes 786440 | tf_op jit(solution)/shard_map/ppermute | solution.py:60
  124.4 12.9 %all-to-all-start.1 = ((bf16[16,16,512]{2,1,0:T(8,128)(2,1)}), bf16[16,16,512]{2,1,0:T(8,128)(2,1)S(1)}, u32[]{:S(2)}, u32[]{:S(2)}) async-start(bf16[16,16,512]{2,1,0:T(8,128)(2,1)} %bitcast.6), calls=%async_computation.1 | async-start | bytes 524288 | tf_op jit(solution)/shard_map/all_to_all | solution.py:416
  (14 other events, 101.5 us)
